TPU v7x, 512 devices: a whole 4x4x16 slice. The times are simulated.
512 devices in a mesh: seq: 64 (over z, y), pipe: 8 (over x, core).
Axes of the slice: x: 4, y: 4, z: 16, core: 2. Of those that a mesh axis runs over, the one named last changes fastest.
Arguments:
- fresh_input: bfloat16 [384, 8192], P(None, 'seq'), may hold values from -8 to 8
- act_prev: bfloat16 [8, 384, 8192], P('pipe', None, 'seq'), may hold values from -8 to 8
- saved_input: bfloat16 [8, 384, 8192], P('pipe', None, 'seq'), may hold values from -8 to 8
- grad_next: bfloat16 [8, 128, 8192], P('pipe', None, 'seq'), may hold values from -8 to 8
- top_grad: bfloat16 [128, 8192], P(None, 'seq'), may hold values from -8 to 8
- filters: float32 [8, 128, 8192], P('pipe', None, 'seq'), may hold values from -0.0625 to 0.0625
Outputs:
- act_next: bfloat16 [8, 128, 8192], P('pipe', None, 'seq')
- grad_input: bfloat16 [8, 384, 8192], P('pipe', None, 'seq')
- filter_grad: float32 [8, 128, 8192], P('pipe', None, 'seq')
All inputs are finite; a program needn't handle non-finite values.
Results may differ from a plain program's by a relative error of at most 0.015.
Values may be sent and summed in bfloat16 or wider, within the bound.
No kernel may reach another device: no remote copies, remote signals or barrier semaphores. Data moves between devices by JAX's collectives and lax.ppermute only.
A program may use at most 64 MiB of HBM per device.

v0:
```python
import math

import jax
import jax.numpy as jnp
from jax import lax
from jax.sharding import PartitionSpec as P

FINEST = lax.Precision.HIGHEST


def from_partner(value, axis, stride):
    mask = 2**stride
    pairs = [(source, source ^ mask) for source in range(lax.axis_size(axis))]
    return lax.ppermute(value, axis, pairs)


def from_behind(x, axis, by):
    length = lax.axis_size(axis)
    pairs = [(i, i + by) for i in range(length) if 0 <= i + by < length]
    return lax.ppermute(x, axis, pairs)


def turn_table(span_len, direction):
    steps_ix = jnp.arange(span_len, dtype=jnp.int32)
    phases = steps_ix[:, None] * steps_ix[None, :] % span_len
    angles = phases.astype(jnp.float32) * (direction * 2.0 * math.pi / span_len)
    return (jnp.cos(angles), jnp.sin(angles))


def complex_einsum(pattern, packed, table_re, table_im):
    real_part = jnp.einsum(pattern, packed[0], table_re, precision=FINEST) - jnp.einsum(
        pattern, packed[1], table_im, precision=FINEST
    )
    imag_part = jnp.einsum(pattern, packed[0], table_im, precision=FINEST) + jnp.einsum(
        pattern, packed[1], table_re, precision=FINEST
    )
    return jnp.stack([real_part, imag_part])


def rotate(packed, angles):
    cosine = jnp.cos(angles)
    sine_part = jnp.sin(angles)
    return jnp.stack(
        [packed[0] * cosine - packed[1] * sine_part, packed[0] * sine_part + packed[1] * cosine]
    )


def product_of(former, latter):
    return jnp.stack(
        [
            former[0] * latter[0] - former[1] * latter[1],
            former[0] * latter[1] + former[1] * latter[0],
        ]
    )


def conj_product(former, latter):
    return jnp.stack(
        [
            former[0] * latter[0] + former[1] * latter[1],
            former[0] * latter[1] - former[1] * latter[0],
        ]
    )


def local_transform(packed, direction):
    full_shape = packed.shape
    seq_width = full_shape[-1]
    inner_len = 128
    outer_len = seq_width // inner_len
    blocks = packed.reshape(full_shape[:-1] + (outer_len, inner_len))
    outer_re, outer_im = turn_table(outer_len, direction)
    inner_re, inner_im = turn_table(inner_len, direction)
    row_ids = jnp.arange(outer_len, dtype=jnp.int32)[:, None]
    col_ids = jnp.arange(inner_len, dtype=jnp.int32)[None, :]
    twiddle = (row_ids * col_ids % seq_width).astype(jnp.float32) * (
        direction * 2.0 * math.pi / seq_width
    )
    if direction < 0:
        blocks = complex_einsum("...jn,jk->...kn", blocks, outer_re, outer_im)
        blocks = rotate(blocks, twiddle)
        blocks = complex_einsum("...kn,nl->...kl", blocks, inner_re, inner_im)
    else:
        blocks = complex_einsum("...kl,ln->...kn", blocks, inner_re, inner_im)
        blocks = rotate(blocks, twiddle)
        blocks = complex_einsum("...kn,kj->...jn", blocks, outer_re, outer_im)
    return blocks.reshape(full_shape)


def levels_forward(packed, dev_index, bit_count):
    for bit_level in reversed(range(bit_count)):
        half_span = 1 << bit_level
        partner = from_partner(packed, "seq", bit_level)
        is_upper = dev_index >> bit_level & 1 == 1
        offset = (dev_index & half_span - 1).astype(jnp.float32)
        low_value = packed + partner
        high_value = rotate(partner - packed, offset * (-math.pi / half_span))
        packed = jnp.where(is_upper, high_value, low_value)
    return packed


def levels_inverse(packed, dev_index, bit_count):
    for bit_level in range(bit_count):
        half_span = 1 << bit_level
        partner = from_partner(packed.astype(jnp.bfloat16), "seq", bit_level).astype(packed.dtype)
        is_upper = dev_index >> bit_level & 1 == 1
        offset = (dev_index & half_span - 1).astype(jnp.float32)
        angles = offset * (math.pi / half_span)
        low_value = packed + rotate(partner, angles)
        high_value = partner - rotate(packed, angles)
        packed = jnp.where(is_upper, high_value, low_value)
    return packed


def held_block(dev_index, bit_count):
    reverse_ix = jnp.zeros_like(dev_index)
    for bit_level in range(bit_count):
        reverse_ix = reverse_ix | (dev_index >> bit_level & 1) << bit_count - 1 - bit_level
    return reverse_ix


def cross_devices(packed, direction):
    dev_count = lax.axis_size("seq")
    dev_index = lax.axis_index("seq")
    bit_count = dev_count.bit_length() - 1
    if direction < 0:
        return levels_forward(packed, dev_index, bit_count)
    return levels_inverse(packed, dev_index, bit_count)


def seq_twist(packed, direction):
    dev_count = lax.axis_size("seq")
    dev_index = lax.axis_index("seq")
    bit_count = dev_count.bit_length() - 1
    seq_width = packed.shape[-1]
    span_total = 2 * seq_width * dev_count
    held = held_block(dev_index, bit_count)
    parity = jnp.arange(2, dtype=jnp.int32)[:, None, None]
    frequency = 2 * held + parity
    position = jnp.arange(seq_width, dtype=jnp.int32)[None, None, :]
    phases = (position * frequency % span_total).astype(jnp.float32) * (
        direction * 2.0 * math.pi / span_total
    )
    return rotate(packed, phases)


def forward_spectrum(signals):
    dev_count = lax.axis_size("seq")
    dev_index = lax.axis_index("seq")
    angles = dev_index.astype(jnp.float32) * (-math.pi / dev_count)
    real_part = jnp.stack([signals, signals * jnp.cos(angles)], axis=1)
    imag_part = jnp.stack([jnp.zeros_like(signals), signals * jnp.sin(angles)], axis=1)
    packed = jnp.stack([real_part, imag_part])
    packed = cross_devices(packed, -1.0)
    packed = seq_twist(packed, -1.0)
    return local_transform(packed, -1.0)


def inverse_signal(packed):
    dev_count = lax.axis_size("seq")
    dev_index = lax.axis_index("seq")
    seq_width = packed.shape[-1]
    packed = local_transform(packed, 1.0)
    packed = seq_twist(packed, 1.0)
    packed = cross_devices(packed, 1.0)
    angles = dev_index.astype(jnp.float32) * (math.pi / dev_count)
    summed = packed[:, :, 0] + rotate(packed[:, :, 1], angles)
    return summed * (1.0 / (2 * seq_width * dev_count))


def per_device(fresh_input, act_prev, saved_input, grad_next, top_grad, filters):
    segments = lax.axis_size("pipe")
    segment_ix = lax.axis_index("pipe")
    arrived = from_behind(act_prev, "pipe", 1)
    returned = from_behind(grad_next, "pipe", -1)
    source = jnp.where(segment_ix == 0, fresh_input, arrived[0]).astype(jnp.float32)
    upstream = jnp.where(segment_ix == segments - 1, top_grad, returned[0]).astype(jnp.float32)
    stored = saved_input[0].astype(jnp.float32)
    kernel = filters[0]
    channels = kernel.shape[0]
    query_fwd = source[:channels]
    mix_fwd = source[channels : 2 * channels] * source[2 * channels :]
    query_bwd = stored[:channels]
    key_bwd = stored[channels : 2 * channels]
    value_bwd = stored[2 * channels :]
    mix_bwd = key_bwd * value_bwd
    spectra = forward_spectrum(jnp.stack([kernel, mix_fwd, mix_bwd]))
    kernel_spec = spectra[:, 0]
    mix_spec = spectra[:, 2]
    conv_a = product_of(kernel_spec, spectra[:, 1])
    conv_b = product_of(kernel_spec, mix_spec)
    conv_out = inverse_signal(jnp.stack([conv_a, conv_b], axis=1))
    conv_fwd = conv_out[0, 0]
    conv_bwd = conv_out[0, 1]
    act_next = (query_fwd * conv_fwd).astype(jnp.bfloat16)
    grad_query = upstream * conv_bwd
    grad_conv = upstream * query_bwd
    grad_spec = forward_spectrum(grad_conv[None])[:, 0]
    back_a = conj_product(kernel_spec, grad_spec)
    back_b = conj_product(mix_spec, grad_spec)
    back_out = inverse_signal(jnp.stack([back_a, back_b], axis=1))
    grad_mix = back_out[0, 0]
    filter_grad = back_out[0, 1]
    grad_source = jnp.concatenate([grad_query, grad_mix * value_bwd, grad_mix * key_bwd]).astype(
        jnp.bfloat16
    )
    return (act_next[None], grad_source[None], filter_grad[None])


def solution(mesh):
    placed = (
        P(None, "seq"),
        P("pipe", None, "seq"),
        P("pipe", None, "seq"),
        P("pipe", None, "seq"),
        P(None, "seq"),
        P("pipe", None, "seq"),
    )
    return jax.shard_map(
        per_device,
        mesh=mesh,
        in_specs=placed,
        out_specs=(P("pipe", None, "seq"), P("pipe", None, "seq"), P("pipe", None, "seq")),
        check_vma=False,
    )
```

profile of v0, /device:TPU:6, one launch (start us, length us, event | category | flops | bytes accessed | tf_op | source)
XLA Modules:
  0.0 554.6 jit_solution(4652377461484887297)
XLA Ops:
  7.8 15.7 %collective-permute-start.1 = (f32[2,3,2,128,128]{4,3,2,1,0:T(8,128)S(1)}, f32[2,3,2,128,128]{4,3,2,1,0:T(8,128)S(1)}, u32[]{:S(2)}, u32[]{:S(2)}) collective-permute-start(f32[2,3,2,128,128]{4,3,2,1,0:T(8,128)S(1)} %pad_maximum_fusion), channel_id=1, source_target_pairs={{0,256},{8,264},{16,272},{24,280},{32,288},{40,296},{48,304},{56,3... | collective-permute-start | bytes 2359304 | tf_op jit(solution)/shard_map/ppermute | solution.py:14
  23.7 23.9 %collective-permute-done.1 = f32[2,3,2,128,128]{4,3,2,1,0:T(8,128)S(1)} collective-permute-done((f32[2,3,2,128,128]{4,3,2,1,0:T(8,128)S(1)}, f32[2,3,2,128,128]{4,3,2,1,0:T(8,128)S(1)}, u32[]{:S(2)}, u32[]{:S(2)}) %collective-permute-start.1) | collective-permute-done | bytes 786464 | tf_op jit(solution)/shard_map/ppermute | solution.py:14
  48.8 37.2 %collective-permute-start.2 = (f32[2,3,2,128,128]{4,3,2,1,0:T(8,128)}, f32[2,3,2,128,128]{4,3,2,1,0:T(8,128)S(1)}, u32[]{:S(2)}, u32[]{:S(2)}) collective-permute-start(f32[2,3,2,128,128]{4,3,2,1,0:T(8,128)} %maximum_select_fusion), channel_id=1, source_target_pairs={{0,128},{8,136},{16,144},{24,152},{32,160},{40,168},{48,176},{56,1... | collective-permute-start | bytes 2359304 | tf_op jit(solution)/shard_map/ppermute | solution.py:14
  86.2 71.0 %collective-permute-done.2 = f32[2,3,2,128,128]{4,3,2,1,0:T(8,128)S(1)} collective-permute-done((f32[2,3,2,128,128]{4,3,2,1,0:T(8,128)}, f32[2,3,2,128,128]{4,3,2,1,0:T(8,128)S(1)}, u32[]{:S(2)}, u32[]{:S(2)}) %collective-permute-start.2) | collective-permute-done | bytes 786464 | tf_op jit(solution)/shard_map/ppermute | solution.py:14
  161.8 34.8 %collective-permute-done.3 = f32[2,3,2,128,128]{4,3,2,1,0:T(8,128)S(1)} collective-permute-done((f32[2,3,2,128,128]{4,3,2,1,0:T(8,128)S(1)}, f32[2,3,2,128,128]{4,3,2,1,0:T(8,128)S(1)}, u32[]{:S(2)}, u32[]{:S(2)}) %collective-permute-start.3) | collective-permute-done | bytes 786464 | tf_op jit(solution)/shard_map/ppermute | solution.py:14
  199.0 19.3 %collective-permute-done.4 = f32[2,3,2,128,128]{4,3,2,1,0:T(8,128)S(1)} collective-permute-done((f32[2,3,2,128,128]{4,3,2,1,0:T(8,128)S(1)}, f32[2,3,2,128,128]{4,3,2,1,0:T(8,128)S(1)}, u32[]{:S(2)}, u32[]{:S(2)}) %collective-permute-start.4) | collective-permute-done | bytes 786464 | tf_op jit(solution)/shard_map/ppermute | solution.py:14
  223.9 16.8 %collective-permute-done.5 = f32[2,3,2,128,128]{4,3,2,1,0:T(8,128)S(1)} collective-permute-done((f32[2,3,2,128,128]{4,3,2,1,0:T(8,128)S(1)}, f32[2,3,2,128,128]{4,3,2,1,0:T(8,128)S(1)}, u32[]{:S(2)}, u32[]{:S(2)}) %collective-permute-start.5) | collective-permute-done | bytes 786464 | tf_op jit(solution)/shard_map/ppermute | solution.py:14
  244.6 15.9 %collective-permute-done.6 = f32[2,3,2,128,128]{4,3,2,1,0:T(8,128)S(1)} collective-permute-done((f32[2,3,2,128,128]{4,3,2,1,0:T(8,128)S(1)}, f32[2,3,2,128,128]{4,3,2,1,0:T(8,128)S(1)}, u32[]{:S(2)}, u32[]{:S(2)}) %collective-permute-start.6) | collective-permute-done | bytes 786464 | tf_op jit(solution)/shard_map/ppermute | solution.py:14
  288.5 5.9 %collective-permute-done.9 = bf16[2,2,2,128,128]{4,3,1,2,0:T(8,128)(2,1)S(1)} collective-permute-done((bf16[2,2,2,128,128]{4,3,1,2,0:T(8,128)(2,1)S(1)}, bf16[2,2,2,128,128]{4,3,1,2,0:T(8,128)(2,1)S(1)}, u32[]{:S(2)}, u32[]{:S(2)}) %collective-permute-start.9) | collective-permute-done | bytes 262176 | tf_op jit(solution)/shard_map/ppermute | solution.py:14
  296.8 10.2 %collective-permute-done.10 = bf16[2,2,2,128,128]{4,3,1,2,0:T(8,128)(2,1)S(1)} collective-permute-done((bf16[2,2,2,128,128]{4,3,1,2,0:T(8,128)(2,1)S(1)}, bf16[2,2,2,128,128]{4,3,1,2,0:T(8,128)(2,1)S(1)}, u32[]{:S(2)}, u32[]{:S(2)}) %collective-permute-start.10) | collective-permute-done | bytes 262176 | tf_op jit(solution)/shard_map/ppermute | solution.py:14
  309.6 24.7 %collective-permute-done.11 = bf16[2,2,2,128,128]{4,3,1,2,0:T(8,128)(2,1)S(1)} collective-permute-done((bf16[2,2,2,128,128]{4,3,1,2,0:T(8,128)(2,1)S(1)}, bf16[2,2,2,128,128]{4,3,1,2,0:T(8,128)(2,1)S(1)}, u32[]{:S(2)}, u32[]{:S(2)}) %collective-permute-start.11) | collective-permute-done | bytes 262176 | tf_op jit(solution)/shard_map/ppermute | solution.py:14
  334.6 12.7 %collective-permute-start.12 = (bf16[2,2,2,128,128]{4,3,1,2,0:T(8,128)(2,1)S(1)}, bf16[2,2,2,128,128]{4,3,1,2,0:T(8,128)(2,1)S(1)}, u32[]{:S(2)}, u32[]{:S(2)}) collective-permute-start(bf16[2,2,2,128,128]{4,3,1,2,0:T(8,128)(2,1)S(1)} %copy.208), channel_id=1, source_target_pairs={{0,256},{8,264},{16,272},{24,280},{32,288},{40,296},{48,304},{56,3... | collective-permute-start | bytes 786440 | tf_op jit(solution)/shard_map/ppermute | solution.py:14
  349.6 7.5 %collective-permute-done.12 = bf16[2,2,2,128,128]{4,3,1,2,0:T(8,128)(2,1)S(1)} collective-permute-done((bf16[2,2,2,128,128]{4,3,1,2,0:T(8,128)(2,1)S(1)}, bf16[2,2,2,128,128]{4,3,1,2,0:T(8,128)(2,1)S(1)}, u32[]{:S(2)}, u32[]{:S(2)}) %collective-permute-start.12) | collective-permute-done | bytes 262176 | tf_op jit(solution)/shard_map/ppermute | solution.py:14
  358.9 7.9 %collective-permute-start.14 = (f32[2,1,2,128,128]{4,3,2,1,0:T(8,128)S(1)}, f32[2,1,2,128,128]{4,3,2,1,0:T(8,128)S(1)}, u32[]{:S(2)}, u32[]{:S(2)}) collective-permute-start(f32[2,1,2,128,128]{4,3,2,1,0:T(8,128)S(1)} %pad_maximum_fusion.10), channel_id=1, source_target_pairs={{0,256},{8,264},{16,272},{24,280},{32,288},{40,296},{48,304},{56,3... | collective-permute-start | bytes 786440 | tf_op jit(solution)/shard_map/ppermute | solution.py:14
  366.8 17.3 %collective-permute-done.14 = f32[2,1,2,128,128]{4,3,2,1,0:T(8,128)S(1)} collective-permute-done((f32[2,1,2,128,128]{4,3,2,1,0:T(8,128)S(1)}, f32[2,1,2,128,128]{4,3,2,1,0:T(8,128)S(1)}, u32[]{:S(2)}, u32[]{:S(2)}) %collective-permute-start.14) | collective-permute-done | bytes 262176 | tf_op jit(solution)/shard_map/ppermute | solution.py:14
  386.1 20.2 %collective-permute-done.15 = f32[2,1,2,128,128]{4,3,2,1,0:T(8,128)S(1)} collective-permute-done((f32[2,1,2,128,128]{4,3,2,1,0:T(8,128)S(1)}, f32[2,1,2,128,128]{4,3,2,1,0:T(8,128)S(1)}, u32[]{:S(2)}, u32[]{:S(2)}) %collective-permute-start.15) | collective-permute-done | bytes 262176 | tf_op jit(solution)/shard_map/ppermute | solution.py:14
  408.5 9.0 %collective-permute-done.16 = f32[2,1,2,128,128]{4,3,2,1,0:T(8,128)S(1)} collective-permute-done((f32[2,1,2,128,128]{4,3,2,1,0:T(8,128)S(1)}, f32[2,1,2,128,128]{4,3,2,1,0:T(8,128)S(1)}, u32[]{:S(2)}, u32[]{:S(2)}) %collective-permute-start.16) | collective-permute-done | bytes 262176 | tf_op jit(solution)/shard_map/ppermute | solution.py:14
  427.8 6.5 %collective-permute-start.18 = (f32[2,1,2,128,128]{4,3,2,1,0:T(8,128)S(1)}, f32[2,1,2,128,128]{4,3,2,1,0:T(8,128)S(1)}, u32[]{:S(2)}, u32[]{:S(2)}) collective-permute-start(f32[2,1,2,128,128]{4,3,2,1,0:T(8,128)S(1)} %maximum_select_fusion.9), channel_id=1, source_target_pairs={{0,16},{8,24},{16,0},{24,8},{32,48},{40,56},{48,32},{56,40},{64,80... | collective-permute-start | bytes 786440 | tf_op jit(solution)/shard_map/ppermute | solution.py:14
  456.2 7.7 %collective-permute-done.20 = bf16[2,2,2,128,128]{4,3,1,2,0:T(8,128)(2,1)S(1)} collective-permute-done((bf16[2,2,2,128,128]{4,3,1,2,0:T(8,128)(2,1)S(1)}, bf16[2,2,2,128,128]{4,3,1,2,0:T(8,128)(2,1)S(1)}, u32[]{:S(2)}, u32[]{:S(2)}) %collective-permute-start.20) | collective-permute-done | bytes 262176 | tf_op jit(solution)/shard_map/ppermute | solution.py:14
  478.3 6.4 %collective-permute-done.22 = bf16[2,2,2,128,128]{4,3,1,2,0:T(8,128)(2,1)S(1)} collective-permute-done((bf16[2,2,2,128,128]{4,3,1,2,0:T(8,128)(2,1)S(1)}, bf16[2,2,2,128,128]{4,3,1,2,0:T(8,128)(2,1)S(1)}, u32[]{:S(2)}, u32[]{:S(2)}) %collective-permute-start.22) | collective-permute-done | bytes 262176 | tf_op jit(solution)/shard_map/ppermute | solution.py:14
  489.9 10.7 %collective-permute-done.23 = bf16[2,2,2,128,128]{4,3,1,2,0:T(8,128)(2,1)S(1)} collective-permute-done((bf16[2,2,2,128,128]{4,3,1,2,0:T(8,128)(2,1)S(1)}, bf16[2,2,2,128,128]{4,3,1,2,0:T(8,128)(2,1)S(1)}, u32[]{:S(2)}, u32[]{:S(2)}) %collective-permute-start.23) | collective-permute-done | bytes 262176 | tf_op jit(solution)/shard_map/ppermute | solution.py:14
  505.7 25.8 %collective-permute-done.24 = bf16[2,2,2,128,128]{4,3,1,2,0:T(8,128)(2,1)S(1)} collective-permute-done((bf16[2,2,2,128,128]{4,3,1,2,0:T(8,128)(2,1)S(1)}, bf16[2,2,2,128,128]{4,3,1,2,0:T(8,128)(2,1)S(1)}, u32[]{:S(2)}, u32[]{:S(2)}) %collective-permute-start.24) | collective-permute-done | bytes 262176 | tf_op jit(solution)/shard_map/ppermute | solution.py:14
  531.7 8.3 %collective-permute-start.25 = (bf16[2,2,2,128,128]{4,3,1,2,0:T(8,128)(2,1)S(1)}, bf16[2,2,2,128,128]{4,3,1,2,0:T(8,128)(2,1)S(1)}, u32[]{:S(2)}, u32[]{:S(2)}) collective-permute-start(bf16[2,2,2,128,128]{4,3,1,2,0:T(8,128)(2,1)S(1)} %get-tuple-element.5), channel_id=1, source_target_pairs={{0,256},{8,264},{16,272},{24,280},{32,288},{40,296},{48,304},{56,3... | collective-permute-start | bytes 786440 | tf_op jit(solution)/shard_map/ppermute | solution.py:14
  540.0 13.0 %collective-permute-done.25 = bf16[2,2,2,128,128]{4,3,1,2,0:T(8,128)(2,1)S(1)} collective-permute-done((bf16[2,2,2,128,128]{4,3,1,2,0:T(8,128)(2,1)S(1)}, bf16[2,2,2,128,128]{4,3,1,2,0:T(8,128)(2,1)S(1)}, u32[]{:S(2)}, u32[]{:S(2)}) %collective-permute-start.25) | collective-permute-done | bytes 262176 | tf_op jit(solution)/shard_map/ppermute | solution.py:14
  (182 shorter events, 122.4 us)
Async XLA Ops:
  7.8 39.8 %collective-permute-start.1 = (f32[2,3,2,128,128]{4,3,2,1,0:T(8,128)S(1)}, f32[2,3,2,128,128]{4,3,2,1,0:T(8,128)S(1)}, u32[]{:S(2)}, u32[]{:S(2)}) collective-permute-start(f32[2,3,2,128,128]{4,3,2,1,0:T(8,128)S(1)} %pad_maximum_fusion), channel_id=1, source_target_pairs={{0,256},{8,264},{16,272},{24,280},{32,288},{40,296},{48,304},{56,3... | collective-permute-start | bytes 2359304 | tf_op jit(solution)/shard_map/ppermute | solution.py:14
  48.8 108.5 %collective-permute-start.2 = (f32[2,3,2,128,128]{4,3,2,1,0:T(8,128)}, f32[2,3,2,128,128]{4,3,2,1,0:T(8,128)S(1)}, u32[]{:S(2)}, u32[]{:S(2)}) collective-permute-start(f32[2,3,2,128,128]{4,3,2,1,0:T(8,128)} %maximum_select_fusion), channel_id=1, source_target_pairs={{0,128},{8,136},{16,144},{24,152},{32,160},{40,168},{48,176},{56,1... | collective-permute-start | bytes 2359304 | tf_op jit(solution)/shard_map/ppermute | solution.py:14
  159.7 36.9 %collective-permute-start.3 = (f32[2,3,2,128,128]{4,3,2,1,0:T(8,128)S(1)}, f32[2,3,2,128,128]{4,3,2,1,0:T(8,128)S(1)}, u32[]{:S(2)}, u32[]{:S(2)}) collective-permute-start(f32[2,3,2,128,128]{4,3,2,1,0:T(8,128)S(1)} %maximum_select_fusion.1), channel_id=1, source_target_pairs={{0,64},{8,72},{16,80},{24,88},{32,96},{40,104},{48,112},{56,120},{... | collective-permute-start | bytes 2359304 | tf_op jit(solution)/shard_map/ppermute | solution.py:14
  196.9 21.4 %collective-permute-start.4 = (f32[2,3,2,128,128]{4,3,2,1,0:T(8,128)S(1)}, f32[2,3,2,128,128]{4,3,2,1,0:T(8,128)S(1)}, u32[]{:S(2)}, u32[]{:S(2)}) collective-permute-start(f32[2,3,2,128,128]{4,3,2,1,0:T(8,128)S(1)} %maximum_select_fusion.2), channel_id=1, source_target_pairs={{0,32},{8,40},{16,48},{24,56},{32,0},{40,8},{48,16},{56,24},{64,96... | collective-permute-start | bytes 2359304 | tf_op jit(solution)/shard_map/ppermute | solution.py:14
  218.6 22.0 %collective-permute-start.5 = (f32[2,3,2,128,128]{4,3,2,1,0:T(8,128)S(1)}, f32[2,3,2,128,128]{4,3,2,1,0:T(8,128)S(1)}, u32[]{:S(2)}, u32[]{:S(2)}) collective-permute-start(f32[2,3,2,128,128]{4,3,2,1,0:T(8,128)S(1)} %maximum_select_fusion.3), channel_id=1, source_target_pairs={{0,16},{8,24},{16,0},{24,8},{32,48},{40,56},{48,32},{56,40},{64,80... | collective-permute-start | bytes 2359304 | tf_op jit(solution)/shard_map/ppermute | solution.py:14
  240.9 19.6 %collective-permute-start.6 = (f32[2,3,2,128,128]{4,3,2,1,0:T(8,128)S(1)}, f32[2,3,2,128,128]{4,3,2,1,0:T(8,128)S(1)}, u32[]{:S(2)}, u32[]{:S(2)}) collective-permute-start(f32[2,3,2,128,128]{4,3,2,1,0:T(8,128)S(1)} %maximum_select_fusion.4), channel_id=1, source_target_pairs={{0,8},{8,0},{16,24},{24,16},{32,40},{40,32},{48,56},{56,48},{64,72... | collective-permute-start | bytes 2359304 | tf_op jit(solution)/shard_map/ppermute | solution.py:14
  266.9 8.3 %collective-permute-start.7 = (bf16[2,2,2,128,128]{4,3,1,2,0:T(8,128)(2,1)S(1)}, bf16[2,2,2,128,128]{4,3,1,2,0:T(8,128)(2,1)S(1)}, u32[]{:S(2)}, u32[]{:S(2)}) collective-permute-start(bf16[2,2,2,128,128]{4,3,1,2,0:T(8,128)(2,1)S(1)} %fusion.10), channel_id=1, source_target_pairs={{0,8},{8,0},{16,24},{24,16},{32,40},{40,32},{48,56},{56,48},{64,72... | collective-permute-start | bytes 786440 | tf_op jit(solution)/shard_map/ppermute | solution.py:14
  275.4 9.8 %collective-permute-start.8 = (bf16[2,2,2,128,128]{4,3,1,2,0:T(8,128)(2,1)S(1)}, bf16[2,2,2,128,128]{4,3,1,2,0:T(8,128)(2,1)S(1)}, u32[]{:S(2)}, u32[]{:S(2)}) collective-permute-start(bf16[2,2,2,128,128]{4,3,1,2,0:T(8,128)(2,1)S(1)} %copy.212), channel_id=1, source_target_pairs={{0,16},{8,24},{16,0},{24,8},{32,48},{40,56},{48,32},{56,40},{64,80... | collective-permute-start | bytes 786440 | tf_op jit(solution)/shard_map/ppermute | solution.py:14
  285.4 9.0 %collective-permute-start.9 = (bf16[2,2,2,128,128]{4,3,1,2,0:T(8,128)(2,1)S(1)}, bf16[2,2,2,128,128]{4,3,1,2,0:T(8,128)(2,1)S(1)}, u32[]{:S(2)}, u32[]{:S(2)}) collective-permute-start(bf16[2,2,2,128,128]{4,3,1,2,0:T(8,128)(2,1)S(1)} %copy.211), channel_id=1, source_target_pairs={{0,32},{8,40},{16,48},{24,56},{32,0},{40,8},{48,16},{56,24},{64,96... | collective-permute-start | bytes 786440 | tf_op jit(solution)/shard_map/ppermute | solution.py:14
  294.7 12.3 %collective-permute-start.10 = (bf16[2,2,2,128,128]{4,3,1,2,0:T(8,128)(2,1)S(1)}, bf16[2,2,2,128,128]{4,3,1,2,0:T(8,128)(2,1)S(1)}, u32[]{:S(2)}, u32[]{:S(2)}) collective-permute-start(bf16[2,2,2,128,128]{4,3,1,2,0:T(8,128)(2,1)S(1)} %copy.210), channel_id=1, source_target_pairs={{0,64},{8,72},{16,80},{24,88},{32,96},{40,104},{48,112},{56,120},{... | collective-permute-start | bytes 786440 | tf_op jit(solution)/shard_map/ppermute | solution.py:14
  307.3 27.1 %collective-permute-start.11 = (bf16[2,2,2,128,128]{4,3,1,2,0:T(8,128)(2,1)S(1)}, bf16[2,2,2,128,128]{4,3,1,2,0:T(8,128)(2,1)S(1)}, u32[]{:S(2)}, u32[]{:S(2)}) collective-permute-start(bf16[2,2,2,128,128]{4,3,1,2,0:T(8,128)(2,1)S(1)} %copy.209), channel_id=1, source_target_pairs={{0,128},{8,136},{16,144},{24,152},{32,160},{40,168},{48,176},{56,1... | collective-permute-start | bytes 786440 | tf_op jit(solution)/shard_map/ppermute | solution.py:14
  334.6 22.6 %collective-permute-start.12 = (bf16[2,2,2,128,128]{4,3,1,2,0:T(8,128)(2,1)S(1)}, bf16[2,2,2,128,128]{4,3,1,2,0:T(8,128)(2,1)S(1)}, u32[]{:S(2)}, u32[]{:S(2)}) collective-permute-start(bf16[2,2,2,128,128]{4,3,1,2,0:T(8,128)(2,1)S(1)} %copy.208), channel_id=1, source_target_pairs={{0,256},{8,264},{16,272},{24,280},{32,288},{40,296},{48,304},{56,3... | collective-permute-start | bytes 786440 | tf_op jit(solution)/shard_map/ppermute | solution.py:14
  347.3 10.2 %collective-permute-start.13 = (bf16[1,128,128]{2,1,0:T(8,128)(2,1)S(1)}, bf16[1,128,128]{2,1,0:T(8,128)(2,1)S(1)}, u32[]{:S(2)}, u32[]{:S(2)}) collective-permute-start(bf16[1,128,128]{2,1,0:T(8,128)(2,1)S(1)} %copy-done.4), channel_id=1, source_target_pairs={{1,0},{2,1},{3,2},{4,3},{5,4},{6,5},{7,6},{9,8},{10,9},{11,10},{12... | collective-permute-start | bytes 98312 | tf_op jit(solution)/shard_map/ppermute | solution.py:20
  358.9 25.2 %collective-permute-start.14 = (f32[2,1,2,128,128]{4,3,2,1,0:T(8,128)S(1)}, f32[2,1,2,128,128]{4,3,2,1,0:T(8,128)S(1)}, u32[]{:S(2)}, u32[]{:S(2)}) collective-permute-start(f32[2,1,2,128,128]{4,3,2,1,0:T(8,128)S(1)} %pad_maximum_fusion.10), channel_id=1, source_target_pairs={{0,256},{8,264},{16,272},{24,280},{32,288},{40,296},{48,304},{56,3... | collective-permute-start | bytes 786440 | tf_op jit(solution)/shard_map/ppermute | solution.py:14
  384.2 22.2 %collective-permute-start.15 = (f32[2,1,2,128,128]{4,3,2,1,0:T(8,128)S(1)}, f32[2,1,2,128,128]{4,3,2,1,0:T(8,128)S(1)}, u32[]{:S(2)}, u32[]{:S(2)}) collective-permute-start(f32[2,1,2,128,128]{4,3,2,1,0:T(8,128)S(1)} %maximum_select_fusion.6), channel_id=1, source_target_pairs={{0,128},{8,136},{16,144},{24,152},{32,160},{40,168},{48,176},{56,1... | collective-permute-start | bytes 786440 | tf_op jit(solution)/shard_map/ppermute | solution.py:14
  406.6 10.9 %collective-permute-start.16 = (f32[2,1,2,128,128]{4,3,2,1,0:T(8,128)S(1)}, f32[2,1,2,128,128]{4,3,2,1,0:T(8,128)S(1)}, u32[]{:S(2)}, u32[]{:S(2)}) collective-permute-start(f32[2,1,2,128,128]{4,3,2,1,0:T(8,128)S(1)} %maximum_select_fusion.7), channel_id=1, source_target_pairs={{0,64},{8,72},{16,80},{24,88},{32,96},{40,104},{48,112},{56,120},{... | collective-permute-start | bytes 786440 | tf_op jit(solution)/shard_map/ppermute | solution.py:14
  417.6 10.0 %collective-permute-start.17 = (f32[2,1,2,128,128]{4,3,2,1,0:T(8,128)S(1)}, f32[2,1,2,128,128]{4,3,2,1,0:T(8,128)S(1)}, u32[]{:S(2)}, u32[]{:S(2)}) collective-permute-start(f32[2,1,2,128,128]{4,3,2,1,0:T(8,128)S(1)} %maximum_select_fusion.8), channel_id=1, source_target_pairs={{0,32},{8,40},{16,48},{24,56},{32,0},{40,8},{48,16},{56,24},{64,96... | collective-permute-start | bytes 786440 | tf_op jit(solution)/shard_map/ppermute | solution.py:14
  427.8 11.9 %collective-permute-start.18 = (f32[2,1,2,128,128]{4,3,2,1,0:T(8,128)S(1)}, f32[2,1,2,128,128]{4,3,2,1,0:T(8,128)S(1)}, u32[]{:S(2)}, u32[]{:S(2)}) collective-permute-start(f32[2,1,2,128,128]{4,3,2,1,0:T(8,128)S(1)} %maximum_select_fusion.9), channel_id=1, source_target_pairs={{0,16},{8,24},{16,0},{24,8},{32,48},{40,56},{48,32},{56,40},{64,80... | collective-permute-start | bytes 786440 | tf_op jit(solution)/shard_map/ppermute | solution.py:14
  453.2 10.8 %collective-permute-start.20 = (bf16[2,2,2,128,128]{4,3,1,2,0:T(8,128)(2,1)S(1)}, bf16[2,2,2,128,128]{4,3,1,2,0:T(8,128)(2,1)S(1)}, u32[]{:S(2)}, u32[]{:S(2)}) collective-permute-start(bf16[2,2,2,128,128]{4,3,1,2,0:T(8,128)(2,1)S(1)} %fusion.9), channel_id=1, source_target_pairs={{0,8},{8,0},{16,24},{24,16},{32,40},{40,32},{48,56},{56,48},{64,72... | collective-permute-start | bytes 786440 | tf_op jit(solution)/shard_map/ppermute | solution.py:14
  464.2 10.2 %collective-permute-start.21 = (bf16[2,2,2,128,128]{4,3,1,2,0:T(8,128)(2,1)S(1)}, bf16[2,2,2,128,128]{4,3,1,2,0:T(8,128)(2,1)S(1)}, u32[]{:S(2)}, u32[]{:S(2)}) collective-permute-start(bf16[2,2,2,128,128]{4,3,1,2,0:T(8,128)(2,1)S(1)} %get-tuple-element.13), channel_id=1, source_target_pairs={{0,16},{8,24},{16,0},{24,8},{32,48},{40,56},{48,32},{56,40},{64,80... | collective-permute-start | bytes 786440 | tf_op jit(solution)/shard_map/ppermute | solution.py:14
  474.5 10.1 %collective-permute-start.22 = (bf16[2,2,2,128,128]{4,3,1,2,0:T(8,128)(2,1)S(1)}, bf16[2,2,2,128,128]{4,3,1,2,0:T(8,128)(2,1)S(1)}, u32[]{:S(2)}, u32[]{:S(2)}) collective-permute-start(bf16[2,2,2,128,128]{4,3,1,2,0:T(8,128)(2,1)S(1)} %get-tuple-element.11), channel_id=1, source_target_pairs={{0,32},{8,40},{16,48},{24,56},{32,0},{40,8},{48,16},{56,24},{64,96... | collective-permute-start | bytes 786440 | tf_op jit(solution)/shard_map/ppermute | solution.py:14
  484.9 15.7 %collective-permute-start.23 = (bf16[2,2,2,128,128]{4,3,1,2,0:T(8,128)(2,1)S(1)}, bf16[2,2,2,128,128]{4,3,1,2,0:T(8,128)(2,1)S(1)}, u32[]{:S(2)}, u32[]{:S(2)}) collective-permute-start(bf16[2,2,2,128,128]{4,3,1,2,0:T(8,128)(2,1)S(1)} %get-tuple-element.9), channel_id=1, source_target_pairs={{0,64},{8,72},{16,80},{24,88},{32,96},{40,104},{48,112},{56,120},{... | collective-permute-start | bytes 786440 | tf_op jit(solution)/shard_map/ppermute | solution.py:14
  500.8 30.7 %collective-permute-start.24 = (bf16[2,2,2,128,128]{4,3,1,2,0:T(8,128)(2,1)S(1)}, bf16[2,2,2,128,128]{4,3,1,2,0:T(8,128)(2,1)S(1)}, u32[]{:S(2)}, u32[]{:S(2)}) collective-permute-start(bf16[2,2,2,128,128]{4,3,1,2,0:T(8,128)(2,1)S(1)} %get-tuple-element.7), channel_id=1, source_target_pairs={{0,128},{8,136},{16,144},{24,152},{32,160},{40,168},{48,176},{56,1... | collective-permute-start | bytes 786440 | tf_op jit(solution)/shard_map/ppermute | solution.py:14
  531.7 21.3 %collective-permute-start.25 = (bf16[2,2,2,128,128]{4,3,1,2,0:T(8,128)(2,1)S(1)}, bf16[2,2,2,128,128]{4,3,1,2,0:T(8,128)(2,1)S(1)}, u32[]{:S(2)}, u32[]{:S(2)}) collective-permute-start(bf16[2,2,2,128,128]{4,3,1,2,0:T(8,128)(2,1)S(1)} %get-tuple-element.5), channel_id=1, source_target_pairs={{0,256},{8,264},{16,272},{24,280},{32,288},{40,296},{48,304},{56,3... | collective-permute-start | bytes 786440 | tf_op jit(solution)/shard_map/ppermute | solution.py:14
  (7 other events, 33.0 us)
where the time goes:
time: 562 us; the launch traced here: 555 us
  waiting for transfers between devices  372 us (66%)
  starting transfers between devices  155 us (28%)
  other arithmetic  11.3 us (2%)
  matrix products  9.99 us (2%)
    ppermute x24, waiting for transfers between devices, from_partner(): return lax.ppermute(value, axis, pairs)  369 us
    ppermute x24, starting transfers between devices, from_partner(): return lax.ppermute(value, axis, pairs)  151 us
  transfers between devices with their start and end apart: 26, of which 25 were waited for; matrix products, arithmetic and copies ran while one was open for 0% of the time, Pallas kernels for 0%

commit v1 on v0

v1 whole, which is shorter than its diff:
```python
import functools

import jax
import jax.numpy as jnp
import ml_dtypes
import numpy as np
from jax import lax
from jax.experimental import pallas as pl
from jax.experimental.pallas import tpu as pltpu
from jax.sharding import PartitionSpec as P

F32 = jnp.float32
BF16 = jnp.bfloat16
PARAMS = pltpu.CompilerParams(vmem_limit_bytes=8 * 2**20)


def split_table(table):
    high = table.astype(ml_dtypes.bfloat16)
    low = (table - high.astype(np.float64)).astype(ml_dtypes.bfloat16)
    return high, low


@functools.lru_cache(maxsize=None)
def tables(blocks, width):
    length = blocks * width
    freq = np.arange(blocks)[:, None] + 0.25
    outer = 2.0 * np.pi * freq * np.arange(blocks)[None, :] / blocks
    inner = 2.0 * np.pi * (np.arange(width)[:, None] * np.arange(width)[None, :] % width) / width
    twist = 2.0 * np.pi * freq * np.arange(width)[None, :] / length
    cos_i, sin_i = np.cos(inner), np.sin(inner)
    outer_fwd = np.concatenate([np.cos(outer), -np.sin(outer)], axis=0)
    inner_fwd = np.block([[cos_i, -sin_i], [sin_i, cos_i]])
    return (
        *split_table(outer_fwd),
        *split_table(inner_fwd),
        *split_table(inner_fwd.T.copy()),
        *split_table(outer_fwd.T / length),
        np.cos(twist).astype(np.float32),
        np.sin(twist).astype(np.float32),
    )


def halves(value):
    high = value.astype(BF16)
    low = (value - high.astype(F32)).astype(BF16)
    return high, low


def dot(a, b):
    return jnp.dot(a, b, preferred_element_type=F32)


def gather_kernel(arrived, fresh, saved, returned, top, filt, out, rows):
    section = lax.axis_index("pipe")
    last = lax.axis_size("pipe") - 1
    channels = filt.shape[1]
    half = channels // 2
    for part in range(2):
        base = half * part

        def at(ref, group):
            span = pl.ds(group * channels + base, half)
            return (ref[0, span, :] if len(ref.shape) == 3 else ref[span, :]).astype(F32)

        key = jnp.where(section == 0, at(fresh, 1), at(arrived, 1))
        value = jnp.where(section == 0, at(fresh, 2), at(arrived, 2))
        upstream = jnp.where(section == last, at(top, 0), at(returned, 0))
        rows[pl.ds(0 + part, half, stride=8), :] = at(filt, 0)
        rows[pl.ds(2 + part, half, stride=8), :] = at(saved, 1) * at(saved, 2)
        rows[pl.ds(4 + part, half, stride=8), :] = key * value
        rows[pl.ds(6 + part, half, stride=8), :] = upstream * at(saved, 0)
    out[...] = rows[...].astype(BF16)


def convolve_kernel(
    blocks, x, f1h, f1l, f2h, f2l, b2h, b2l, b1h, b1l, cos_t, sin_t, out, rows
):
    rows[...] = x[...].astype(F32)
    taken = [rows[pl.ds(r, blocks, stride=8), :].astype(BF16) for r in range(8)]
    flat = jnp.concatenate(taken, axis=1)
    first = dot(f1h[...], flat) + dot(f1l[...], flat)
    width = x.shape[1]
    cosine, sine = cos_t[...], sin_t[...]
    stacked = []
    for r in range(8):
        real = first[:blocks, r * width : (r + 1) * width]
        imag = first[blocks:, r * width : (r + 1) * width]
        stacked.append(
            jnp.concatenate([real * cosine + imag * sine, imag * cosine - real * sine], axis=1)
        )
    high, low = halves(jnp.concatenate(stacked, axis=0))
    spec = dot(high, f2h[...]) + (dot(high, f2l[...]) + dot(low, f2h[...]))

    def parts_of(r):
        return (
            spec[r * blocks : (r + 1) * blocks, :width],
            spec[r * blocks : (r + 1) * blocks, width:],
        )

    products = []
    for kind in range(4):
        for part in range(2):
            filt, mix_b, mix_f, grad = (parts_of(2 * k + part) for k in range(4))
            if kind < 2:
                (ar, ai), (br, bi) = filt, (mix_f if kind == 0 else mix_b)
                pair = [ar * br - ai * bi, ar * bi + ai * br]
            else:
                (ar, ai), (br, bi) = (filt if kind == 2 else mix_b), grad
                pair = [ar * br + ai * bi, ar * bi - ai * br]
            products.append(jnp.concatenate(pair, axis=1))
    high, low = halves(jnp.concatenate(products, axis=0))
    back = dot(high, b2h[...]) + (dot(high, b2l[...]) + dot(low, b2h[...]))
    columns = []
    for r in range(8):
        real = back[r * blocks : (r + 1) * blocks, :width]
        imag = back[r * blocks : (r + 1) * blocks, width:]
        columns.append(
            jnp.concatenate([real * cosine - imag * sine, imag * cosine + real * sine], axis=0)
        )
    high, low = halves(jnp.concatenate(columns, axis=1))
    last = dot(b1h[...], high) + (dot(b1h[...], low) + dot(b1l[...], high))
    for r in range(8):
        rows[pl.ds(r, blocks, stride=8), :] = last[:, r * width : (r + 1) * width]
    out[...] = rows[...].astype(BF16)


def finish_kernel(x, arrived, fresh, saved, returned, top, act, grad_in, filt_grad, rows):
    section = lax.axis_index("pipe")
    last = lax.axis_size("pipe") - 1
    channels = act.shape[1]
    half = channels // 2
    rows[...] = x[...].astype(F32)
    for part in range(2):
        base = half * part

        def at(ref, group):
            span = pl.ds(group * channels + base, half)
            return (ref[0, span, :] if len(ref.shape) == 3 else ref[span, :]).astype(F32)

        def result(kind):
            return rows[pl.ds(2 * kind + part, half, stride=8), :]

        query = jnp.where(section == 0, at(fresh, 0), at(arrived, 0))
        upstream = jnp.where(section == last, at(top, 0), at(returned, 0))
        grad_mix = result(2)
        act[0, pl.ds(base, half), :] = (query * result(0)).astype(BF16)
        grad_in[0, pl.ds(base, half), :] = (upstream * result(1)).astype(BF16)
        grad_in[0, pl.ds(channels + base, half), :] = (grad_mix * at(saved, 2)).astype(BF16)
        grad_in[0, pl.ds(2 * channels + base, half), :] = (grad_mix * at(saved, 1)).astype(BF16)
        filt_grad[0, pl.ds(base, half), :] = result(3)


def per_device(fresh_input, act_prev, saved_input, grad_next, top_grad, filters):
    sections = lax.axis_size("pipe")
    blocks = lax.axis_size("seq")
    channels, width = filters.shape[1], filters.shape[2]
    total = 4 * channels
    arrived = lax.ppermute(act_prev, "pipe", [(i, i + 1) for i in range(sections - 1)])
    returned = lax.ppermute(grad_next, "pipe", [(i + 1, i) for i in range(sections - 1)])
    scratch = [pltpu.VMEM((total, width), F32)]
    sent = pl.pallas_call(
        gather_kernel,
        out_shape=jax.ShapeDtypeStruct((total, width), BF16),
        scratch_shapes=scratch,
        compiler_params=PARAMS,
        name="gather_rows",
    )(arrived, fresh_input, saved_input, returned, top_grad, filters)

    def trade(value):
        cut = value.reshape(blocks, total // blocks, width)
        return lax.all_to_all(cut, "seq", 0, 0).reshape(total, width)

    held = trade(sent)
    done = pl.pallas_call(
        functools.partial(convolve_kernel, blocks),
        out_shape=jax.ShapeDtypeStruct((total, width), BF16),
        scratch_shapes=scratch,
        compiler_params=PARAMS,
        name="convolve",
    )(held, *(jnp.asarray(t) for t in tables(blocks, width)))
    back = trade(done)
    return pl.pallas_call(
        finish_kernel,
        out_shape=(
            jax.ShapeDtypeStruct((1, channels, width), BF16),
            jax.ShapeDtypeStruct((1, 3 * channels, width), BF16),
            jax.ShapeDtypeStruct((1, channels, width), F32),
        ),
        scratch_shapes=scratch,
        compiler_params=PARAMS,
        name="finish",
    )(back, arrived, fresh_input, saved_input, returned, top_grad)


def solution(mesh):
    placed = (
        P(None, "seq"),
        P("pipe", None, "seq"),
        P("pipe", None, "seq"),
        P("pipe", None, "seq"),
        P(None, "seq"),
        P("pipe", None, "seq"),
    )
    return jax.shard_map(
        per_device,
        mesh=mesh,
        in_specs=placed,
        out_specs=(P("pipe", None, "seq"), P("pipe", None, "seq"), P("pipe", None, "seq")),
        check_vma=False,
    )
```

time: 562 us -> 74.1 us (0.13)
  the two profiles are of different devices: /device:TPU:6 before, /device:TPU:2 now
where the time goes in v1:
time: 74.1 us; the launch traced here: 73.7 us
  blocking collectives  59.6 us (80%)
  starting transfers between devices  5.56 us (8%)
  local copies, waits for them, and re-layouts  3.45 us (5%)
  Pallas kernels  2.35 us (3%)
  waiting for transfers between devices  1.89 us (3%)
  between operations  0.8 us (1%)
    all_to_all x2, blocking collectives, trade(): return lax.all_to_all(cut, 'seq', 0, 0).reshape(total, width)  59.6 us
    ppermute x1, starting transfers between devices, per_device(): lax.ppermute(grad_next, 'pipe', [(i + 1, i) for i in range(sections - 1)])  3.64 us
    unnamed x32, local copies, waits for them, and re-layouts  3.45 us
    ppermute x1, starting transfers between devices, per_device(): lax.ppermute(act_prev, 'pipe', [(i, i + 1) for i in range(sections - 1)])  1.92 us
    ppermute x1, waiting for transfers between devices, per_device(): lax.ppermute(grad_next, 'pipe', [(i + 1, i) for i in range(sections - 1)])  1.89 us
    pallas_call x1, Pallas kernels, per_device(): pl.pallas_call(functools.partial(convolve_kernel, blocks), out_shape=jax....  1.54 us
  transfers between devices with their start and end apart: 2, of which 1 were waited for; matrix products, arithmetic and copies ran while one was open for 0% of the time, Pallas kernels for 0%

profile of v1, /device:TPU:2, one launch (start us, length us, event | category | flops | bytes accessed | tf_op | source)
XLA Modules:
  0.0 73.7 jit_solution(12274955695437006672)
XLA Ops:
  0.6 1.9 %collective-permute-start = (bf16[1,384,128]{2,1,0:T(8,128)(2,1)}, bf16[1,384,128]{2,1,0:T(8,128)(2,1)S(1)}, u32[]{:S(2)}, u32[]{:S(2)}) collective-permute-start(bf16[1,384,128]{2,1,0:T(8,128)(2,1)} %param.17), channel_id=1, source_target_pairs={{0,1},{1,2},{2,3},{3,4},{4,5},{5,6},{6,7},{8,9},{9,10},{10,11},{11... | collective-permute-start | bytes 294920 | tf_op jit(solution)/shard_map/ppermute | solution.py:158
  2.6 3.6 %collective-permute-start.1 = (bf16[1,128,128]{2,1,0:T(8,128)(2,1)}, bf16[1,128,128]{2,1,0:T(8,128)(2,1)S(1)}, u32[]{:S(2)}, u32[]{:S(2)}) collective-permute-start(bf16[1,128,128]{2,1,0:T(8,128)(2,1)} %param.19), channel_id=1, source_target_pairs={{1,0},{2,1},{3,2},{4,3},{5,4},{6,5},{7,6},{9,8},{10,9},{11,10},{12... | collective-permute-start | bytes 98312 | tf_op jit(solution)/shard_map/ppermute | solution.py:159
  6.2 1.9 %collective-permute-done.1.returned = bf16[1,128,128]{2,1,0:T(8,128)(2,1)S(1)} collective-permute-done((bf16[1,128,128]{2,1,0:T(8,128)(2,1)}, bf16[1,128,128]{2,1,0:T(8,128)(2,1)S(1)}, u32[]{:S(2)}, u32[]{:S(2)}) %collective-permute-start.1) | collective-permute-done | bytes 32800 | tf_op jit(solution)/shard_map/ppermute | solution.py:159
  8.1 0.0 collective-permute-done.arrived
  8.1 0.9 %copy-done = bf16[384,128]{1,0:T(8,128)(2,1)S(1)} copy-done((bf16[384,128]{1,0:T(8,128)(2,1)S(1)}, bf16[384,128]{1,0:T(8,128)(2,1)}, u32[]{:S(2)}) %copy-start) | copy-done | bytes 98328
  9.0 0.9 %copy-done.2 = bf16[1,384,128]{2,1,0:T(8,128)(2,1)S(1)} copy-done((bf16[1,384,128]{2,1,0:T(8,128)(2,1)S(1)}, bf16[1,384,128]{2,1,0:T(8,128)(2,1)}, u32[]{:S(2)}) %copy-start.2) | copy-done | bytes 98328
  9.9 0.8 %copy-done.8 = bf16[128,128]{1,0:T(8,128)(2,1)S(1)} copy-done((bf16[128,128]{1,0:T(8,128)(2,1)S(1)}, bf16[128,128]{1,0:T(8,128)(2,1)}, u32[]{:S(2)}) %copy-start.8) | copy-done | bytes 32792
  10.7 0.8 %copy-done.9 = f32[1,128,128]{2,1,0:T(8,128)S(1)} copy-done((f32[1,128,128]{2,1,0:T(8,128)S(1)}, f32[1,128,128]{2,1,0:T(8,128)}, u32[]{:S(2)}) %copy-start.9) | copy-done | bytes 65560
  11.5 0.0 copy-start.12
  11.5 0.0 copy-start.13
  11.5 0.0 copy-start.14
  11.5 0.0 copy-start.15
  11.6 0.1 gather_rows.1
  11.6 0.0 copy-start.4
  11.7 0.0 copy-start.5
  11.7 36.8 %all_to_all.10 = bf16[64,8,128]{2,1,0:T(8,128)(2,1)S(1)} all-to-all(bf16[64,8,128]{2,1,0:T(8,128)(2,1)S(1)} %bitcast.4), channel_id=1, replica_groups=mesh['seq'=64,'pipe'=8] {'seq'}, dimensions={0} | all-to-all | bytes 262144 | tf_op jit(solution)/shard_map/all_to_all | solution.py:171
  48.4 0.0 copy-done.6
  48.4 0.0 copy-done.7
  48.5 1.5 %convolve.1 = bf16[512,128]{1,0:T(8,128)(2,1)S(1)} custom-call(bf16[512,128]{1,0:T(8,128)(2,1)S(1)} %bitcast.6, bf16[128,64]{1,0:T(8,128)(2,1)S(1)} %copy-done.13, bf16[128,64]{1,0:T(8,128)(2,1)S(1)} %copy-done.12, bf16[256,256]{1,0:T(8,128)(2,1)S(1)} %copy-done.7, bf16[256,256]{1,0:T(8,128)(2,1)S(1)} %copy-done.6, bf16[256,256]{1,0:T(8,128)(2,1)S(1)} %copy-done.5, ...), custom_call_target="tpu_custom_call" | custom-call | tf_op jit(solution)/shard_map/convolve/pallas_call | solution.py:174
  50.0 0.0 copy-start.1
  50.1 0.0 copy-start.3
  50.1 22.9 %all_to_all.11 = bf16[64,8,128]{2,1,0:T(8,128)(2,1)S(1)} all-to-all(bf16[64,8,128]{2,1,0:T(8,128)(2,1)S(1)} %bitcast.7), channel_id=1, replica_groups=mesh['seq'=64,'pipe'=8] {'seq'}, dimensions={0} | all-to-all | bytes 262144 | tf_op jit(solution)/shard_map/all_to_all | solution.py:171
  73.0 0.0 copy-done.1
  73.0 0.7 finish.1
  (17 shorter events, 0.0 us)
Async XLA Ops:
  0.6 7.5 %collective-permute-start = (bf16[1,384,128]{2,1,0:T(8,128)(2,1)}, bf16[1,384,128]{2,1,0:T(8,128)(2,1)S(1)}, u32[]{:S(2)}, u32[]{:S(2)}) collective-permute-start(bf16[1,384,128]{2,1,0:T(8,128)(2,1)} %param.17), channel_id=1, source_target_pairs={{0,1},{1,2},{2,3},{3,4},{4,5},{5,6},{6,7},{8,9},{9,10},{10,11},{11... | collective-permute-start | bytes 294920 | tf_op jit(solution)/shard_map/ppermute | solution.py:158
  2.6 5.5 %collective-permute-start.1 = (bf16[1,128,128]{2,1,0:T(8,128)(2,1)}, bf16[1,128,128]{2,1,0:T(8,128)(2,1)S(1)}, u32[]{:S(2)}, u32[]{:S(2)}) collective-permute-start(bf16[1,128,128]{2,1,0:T(8,128)(2,1)} %param.19), channel_id=1, source_target_pairs={{1,0},{2,1},{3,2},{4,3},{5,4},{6,5},{7,6},{9,8},{10,9},{11,10},{12... | collective-permute-start | bytes 98312 | tf_op jit(solution)/shard_map/ppermute | solution.py:159
  8.1 0.9 %copy-start = (bf16[384,128]{1,0:T(8,128)(2,1)S(1)}, bf16[384,128]{1,0:T(8,128)(2,1)}, u32[]{:S(2)}) copy-start(bf16[384,128]{1,0:T(8,128)(2,1)} %fresh.3) | copy-start | bytes 294916
  9.0 0.9 %copy-start.2 = (bf16[1,384,128]{2,1,0:T(8,128)(2,1)S(1)}, bf16[1,384,128]{2,1,0:T(8,128)(2,1)}, u32[]{:S(2)}) copy-start(bf16[1,384,128]{2,1,0:T(8,128)(2,1)} %saved.3) | copy-start | bytes 294916
  9.9 0.8 %copy-start.8 = (bf16[128,128]{1,0:T(8,128)(2,1)S(1)}, bf16[128,128]{1,0:T(8,128)(2,1)}, u32[]{:S(2)}) copy-start(bf16[128,128]{1,0:T(8,128)(2,1)} %top.3) | copy-start | bytes 98308
  10.6 0.8 %copy-start.9 = (f32[1,128,128]{2,1,0:T(8,128)S(1)}, f32[1,128,128]{2,1,0:T(8,128)}, u32[]{:S(2)}) copy-start(f32[1,128,128]{2,1,0:T(8,128)} %filt.1) | copy-start | bytes 196612
  11.5 36.9 %copy-start.6 = (bf16[256,256]{1,0:T(8,128)(2,1)S(1)}, bf16[256,256]{1,0:T(8,128)(2,1)}, u32[]{:S(2)}) copy-start(bf16[256,256]{1,0:T(8,128)(2,1)} %constant.23.clone.f2l) | copy-start | bytes 393220
  11.5 36.9 %copy-start.7 = (bf16[256,256]{1,0:T(8,128)(2,1)S(1)}, bf16[256,256]{1,0:T(8,128)(2,1)}, u32[]{:S(2)}) copy-start(bf16[256,256]{1,0:T(8,128)(2,1)} %constant.22.clone.f2h) | copy-start | bytes 393220
  11.5 36.9 %copy-start.10 = (f32[64,128]{1,0:T(8,128)S(1)}, f32[64,128]{1,0:T(8,128)}, u32[]{:S(2)}) copy-start(f32[64,128]{1,0:T(8,128)} %constant.29.clone.sin_t) | copy-start | bytes 98308
  11.5 36.9 %copy-start.11 = (f32[64,128]{1,0:T(8,128)S(1)}, f32[64,128]{1,0:T(8,128)}, u32[]{:S(2)}) copy-start(f32[64,128]{1,0:T(8,128)} %constant.28.clone.cos_t) | copy-start | bytes 98308
  11.5 36.9 %copy-start.12 = (bf16[128,64]{1,0:T(8,128)(2,1)S(1)}, bf16[128,64]{1,0:T(8,128)(2,1)}, u32[]{:S(2)}) copy-start(bf16[128,64]{1,0:T(8,128)(2,1)} %constant.21.clone.f1l) | copy-start | bytes 49156
  11.5 36.9 %copy-start.13 = (bf16[128,64]{1,0:T(8,128)(2,1)S(1)}, bf16[128,64]{1,0:T(8,128)(2,1)}, u32[]{:S(2)}) copy-start(bf16[128,64]{1,0:T(8,128)(2,1)} %constant.20.clone.f1h) | copy-start | bytes 49156
  11.5 36.9 %copy-start.14 = (bf16[64,128]{1,0:T(8,128)(2,1)S(1)}, bf16[64,128]{1,0:T(8,128)(2,1)}, u32[]{:S(2)}) copy-start(bf16[64,128]{1,0:T(8,128)(2,1)} %constant.27.clone.b1l) | copy-start | bytes 49156
  11.5 36.9 %copy-start.15 = (bf16[64,128]{1,0:T(8,128)(2,1)S(1)}, bf16[64,128]{1,0:T(8,128)(2,1)}, u32[]{:S(2)}) copy-start(bf16[64,128]{1,0:T(8,128)(2,1)} %constant.26.clone.b1h) | copy-start | bytes 49156
  11.6 36.8 %copy-start.4 = (bf16[256,256]{1,0:T(8,128)(2,1)S(1)}, bf16[256,256]{1,0:T(8,128)(2,1)}, u32[]{:S(2)}) copy-start(bf16[256,256]{1,0:T(8,128)(2,1)} %constant.25.clone.b2l) | copy-start | bytes 393220
  11.7 36.8 %copy-start.5 = (bf16[256,256]{1,0:T(8,128)(2,1)S(1)}, bf16[256,256]{1,0:T(8,128)(2,1)}, u32[]{:S(2)}) copy-start(bf16[256,256]{1,0:T(8,128)(2,1)} %constant.24.clone.b2h) | copy-start | bytes 393220
  50.0 22.9 %copy-start.1 = (bf16[384,128]{1,0:T(8,128)(2,1)S(1)}, bf16[384,128]{1,0:T(8,128)(2,1)}, u32[]{:S(2)}) copy-start(bf16[384,128]{1,0:T(8,128)(2,1)} %fresh.3) | copy-start | bytes 294916
  50.1 22.9 %copy-start.3 = (bf16[1,384,128]{2,1,0:T(8,128)(2,1)S(1)}, bf16[1,384,128]{2,1,0:T(8,128)(2,1)}, u32[]{:S(2)}) copy-start(bf16[1,384,128]{2,1,0:T(8,128)(2,1)} %saved.3) | copy-start | bytes 294916

commit v2 on v1

--- a/solution.py
+++ b/solution.py
@@ -20,11 +20,16 @@
     return high, low
 
 
+def trade_order(blocks):
+    first = blocks // 2 + 2 if blocks > 4 else 0
+    return [(first + i) % blocks for i in range(blocks)]
+
+
 @functools.lru_cache(maxsize=None)
 def tables(blocks, width):
     length = blocks * width
     freq = np.arange(blocks)[:, None] + 0.25
-    outer = 2.0 * np.pi * freq * np.arange(blocks)[None, :] / blocks
+    outer = 2.0 * np.pi * freq * np.array(trade_order(blocks))[None, :] / blocks
     inner = 2.0 * np.pi * (np.arange(width)[:, None] * np.arange(width)[None, :] % width) / width
     twist = 2.0 * np.pi * freq * np.arange(width)[None, :] / length
     cos_i, sin_i = np.cos(inner), np.sin(inner)
@@ -48,6 +53,15 @@
 
 def dot(a, b):
     return jnp.dot(a, b, preferred_element_type=F32)
+
+
+def stage_kernel(fresh, saved, top, filt, fresh_v, saved_v, top_v, filt_v, sems):
+    pairs = ((filt, filt_v), (saved, saved_v), (fresh, fresh_v), (top, top_v))
+    copies = [pltpu.make_async_copy(a, b, sems.at[i]) for i, (a, b) in enumerate(pairs)]
+    for copy in copies:
+        copy.start()
+    for copy in copies:
+        copy.wait()
 
 
 def gather_kernel(arrived, fresh, saved, returned, top, filt, out, rows):
@@ -155,8 +169,23 @@
     blocks = lax.axis_size("seq")
     channels, width = filters.shape[1], filters.shape[2]
     total = 4 * channels
-    arrived = lax.ppermute(act_prev, "pipe", [(i, i + 1) for i in range(sections - 1)])
-    returned = lax.ppermute(grad_next, "pipe", [(i + 1, i) for i in range(sections - 1)])
+    ring = [(i, (i + 1) % sections) for i in range(sections)]
+    arrived = lax.ppermute(act_prev, "pipe", ring)
+    returned = lax.ppermute(grad_next, "pipe", [(b, a) for a, b in ring])
+    whole = [
+        pltpu.with_memory_space_constraint(a, pltpu.HBM)
+        for a in (fresh_input, saved_input, top_grad, filters)
+    ]
+    fresh_input, saved_input, top_grad, filters = pl.pallas_call(
+        stage_kernel,
+        out_shape=[jax.ShapeDtypeStruct(a.shape, a.dtype) for a in whole],
+        in_specs=[pl.BlockSpec(memory_space=pltpu.HBM)] * 4,
+        out_specs=[pl.BlockSpec(memory_space=pltpu.VMEM)] * 4,
+        scratch_shapes=[pltpu.SemaphoreType.DMA((4,))],
+        compiler_params=PARAMS,
+        cost_estimate=pl.CostEstimate(flops=0, bytes_accessed=2**19, transcendentals=0),
+        name="stage_inputs",
+    )(*whole)
     scratch = [pltpu.VMEM((total, width), F32)]
     sent = pl.pallas_call(
         gather_kernel,
@@ -166,9 +195,11 @@
         name="gather_rows",
     )(arrived, fresh_input, saved_input, returned, top_grad, filters)
 
+    order = [trade_order(blocks)]
+
     def trade(value):
         cut = value.reshape(blocks, total // blocks, width)
-        return lax.all_to_all(cut, "seq", 0, 0).reshape(total, width)
+        return lax.all_to_all(cut, "seq", 0, 0, axis_index_groups=order).reshape(total, width)
 
     held = trade(sent)
     done = pl.pallas_call(

time: 74.1 us -> 59.4 us (0.80)
  the two profiles are of different devices: /device:TPU:2 before, /device:TPU:6 now
where the time goes in v2:
time: 59.4 us; the launch traced here: 59.2 us
  blocking collectives  49.1 us (83%)
  waiting for transfers between devices  4.11 us (7%)
  Pallas kernels  3.35 us (6%)
  starting transfers between devices  1.75 us (3%)
  between operations  0.79 us (1%)
    all_to_all x2, blocking collectives, trade(): lax.all_to_all(cut, 'seq', 0, 0, axis_index_groups=order)  49.1 us
    ppermute x1, waiting for transfers between devices, per_device(): returned = lax.ppermute(grad_next, 'pipe', [(b, a) for a, b in ring])  4.11 us
    ppermute x1, starting transfers between devices, per_device(): returned = lax.ppermute(grad_next, 'pipe', [(b, a) for a, b in ring])  1.73 us
    pallas_call x1, Pallas kernels, per_device(): pl.pallas_call(functools.partial(convolve_kernel, blocks), out_shape=jax....  1.53 us
  transfers between devices with their start and end apart: 2, of which 1 were waited for; matrix products, arithmetic and copies ran while one was open for 0% of the time, Pallas kernels for 2%

profile of v2, /device:TPU:6, one launch (start us, length us, event | category | flops | bytes accessed | tf_op | source)
XLA Modules:
  0.0 59.2 jit_solution(3091397905936060511)
XLA Ops:
  0.6 0.0 collective-permute-start
  0.7 1.7 %collective-permute-start.1 = (bf16[1,128,128]{2,1,0:T(8,128)(2,1)}, bf16[1,128,128]{2,1,0:T(8,128)(2,1)S(1)}, u32[]{:S(2)}, u32[]{:S(2)}) collective-permute-start(bf16[1,128,128]{2,1,0:T(8,128)(2,1)} %param.19), channel_id=1, source_target_pairs={{1,0},{2,1},{3,2},{4,3},{5,4},{6,5},{7,6},{0,7},{9,8},{10,9},{11,1... | collective-permute-start | bytes 98312 | tf_op jit(solution)/shard_map/ppermute | solution.py:174
  2.4 1.0 %stage_inputs.1 = (bf16[384,128]{1,0:T(8,128)(2,1)S(1)}, bf16[1,384,128]{2,1,0:T(8,128)(2,1)S(1)}, bf16[128,128]{1,0:T(8,128)(2,1)S(1)}, f32[1,128,128]{2,1,0:T(8,128)S(1)}) custom-call(bf16[384,128]{1,0:T(8,128)(2,1)} %fresh.1, bf16[1,384,128]{2,1,0:T(8,128)(2,1)} %saved.1, bf16[128,128]{1,0:T(8,128)(2,1)} %top.1, f32[1,128,128]{2,1,0:T(8,128)} %filt.1), custom_call_target="tpu_custom_call" | custom-call | bytes 524288 | tf_op jit(solution)/shard_map/stage_inputs/pallas_call | solution.py:179
  3.4 4.1 %collective-permute-done.1.returned = bf16[1,128,128]{2,1,0:T(8,128)(2,1)S(1)} collective-permute-done((bf16[1,128,128]{2,1,0:T(8,128)(2,1)}, bf16[1,128,128]{2,1,0:T(8,128)(2,1)S(1)}, u32[]{:S(2)}, u32[]{:S(2)}) %collective-permute-start.1) | collective-permute-done | bytes 32800 | tf_op jit(solution)/shard_map/ppermute | solution.py:174
  7.5 0.0 collective-permute-done.arrived
  7.5 0.0 copy-start.5
  7.5 0.0 copy-start.6
  7.6 0.0 copy-start.7
  7.6 0.0 copy-start.8
  7.6 0.0 copy-start.9
  7.6 0.1 gather_rows.1
  7.7 0.0 copy-start
  7.7 0.0 copy-start.1
  7.7 27.6 %all_to_all.10 = bf16[64,8,128]{2,1,0:T(8,128)(2,1)S(1)} all-to-all(bf16[64,8,128]{2,1,0:T(8,128)(2,1)S(1)} %bitcast.4), channel_id=1, replica_groups={{272,280,288,296,304,312,320,328,336,344,352,360,368,376,384,392,400,40..., dimensions={0} | all-to-all | bytes 262144 | tf_op jit(solution)/shard_map/all_to_all | solution.py:202
  35.4 0.0 copy-done.2
  35.4 0.0 copy-done.3
  35.4 0.0 copy-done.4
  35.4 0.0 copy-done.5
  35.4 0.0 copy-done.6
  35.4 0.0 copy-done.7
  35.4 0.0 copy-done.8
  35.4 1.5 %convolve.1 = bf16[512,128]{1,0:T(8,128)(2,1)S(1)} custom-call(bf16[512,128]{1,0:T(8,128)(2,1)S(1)} %bitcast.6, bf16[128,64]{1,0:T(8,128)(2,1)S(1)} %copy-done.7, bf16[128,64]{1,0:T(8,128)(2,1)S(1)} %copy-done.6, bf16[256,256]{1,0:T(8,128)(2,1)S(1)} %copy-done.3, bf16[256,256]{1,0:T(8,128)(2,1)S(1)} %copy-done.2, bf16[256,256]{1,0:T(8,128)(2,1)S(1)} %copy-done.1, ...), custom_call_target="tpu_custom_call" | custom-call | tf_op jit(solution)/shard_map/convolve/pallas_call | solution.py:205
  37.0 21.5 %all_to_all.11 = bf16[64,8,128]{2,1,0:T(8,128)(2,1)S(1)} all-to-all(bf16[64,8,128]{2,1,0:T(8,128)(2,1)S(1)} %bitcast.7), channel_id=1, replica_groups={{272,280,288,296,304,312,320,328,336,344,352,360,368,376,384,392,400,40..., dimensions={0} | all-to-all | bytes 262144 | tf_op jit(solution)/shard_map/all_to_all | solution.py:202
  58.4 0.7 %finish.1 = (bf16[1,128,128]{2,1,0:T(8,128)(2,1)}, bf16[1,384,128]{2,1,0:T(8,128)(2,1)}, f32[1,128,128]{2,1,0:T(8,128)}) custom-call(bf16[512,128]{1,0:T(8,128)(2,1)S(1)} %bitcast.5, bf16[1,384,128]{2,1,0:T(8,128)(2,1)S(1)} %collective-permute-done.arrived, bf16[384,128]{1,0:T(8,128)(2,1)S(1)} %get-tuple-element.7.fresh, ...), custom_call_target="tpu_custom_call" | custom-call | tf_op jit(solution)/shard_map/finish/pallas_call | solution.py:213
  (6 shorter events, 0.0 us)
Async XLA Ops:
  0.6 6.9 %collective-permute-start = (bf16[1,384,128]{2,1,0:T(8,128)(2,1)}, bf16[1,384,128]{2,1,0:T(8,128)(2,1)S(1)}, u32[]{:S(2)}, u32[]{:S(2)}) collective-permute-start(bf16[1,384,128]{2,1,0:T(8,128)(2,1)} %param.17), channel_id=1, source_target_pairs={{0,1},{1,2},{2,3},{3,4},{4,5},{5,6},{6,7},{7,0},{8,9},{9,10},{10,1... | collective-permute-start | bytes 294920 | tf_op jit(solution)/shard_map/ppermute | solution.py:173
  0.7 6.9 %collective-permute-start.1 = (bf16[1,128,128]{2,1,0:T(8,128)(2,1)}, bf16[1,128,128]{2,1,0:T(8,128)(2,1)S(1)}, u32[]{:S(2)}, u32[]{:S(2)}) collective-permute-start(bf16[1,128,128]{2,1,0:T(8,128)(2,1)} %param.19), channel_id=1, source_target_pairs={{1,0},{2,1},{3,2},{4,3},{5,4},{6,5},{7,6},{0,7},{9,8},{10,9},{11,1... | collective-permute-start | bytes 98312 | tf_op jit(solution)/shard_map/ppermute | solution.py:174
  7.5 27.8 %copy-start.2 = (bf16[256,256]{1,0:T(8,128)(2,1)S(1)}, bf16[256,256]{1,0:T(8,128)(2,1)}, u32[]{:S(2)}) copy-start(bf16[256,256]{1,0:T(8,128)(2,1)} %constant.23.clone.f2l) | copy-start | bytes 393220
  7.5 27.8 %copy-start.3 = (bf16[256,256]{1,0:T(8,128)(2,1)S(1)}, bf16[256,256]{1,0:T(8,128)(2,1)}, u32[]{:S(2)}) copy-start(bf16[256,256]{1,0:T(8,128)(2,1)} %constant.22.clone.f2h) | copy-start | bytes 393220
  7.5 27.8 %copy-start.4 = (f32[64,128]{1,0:T(8,128)S(1)}, f32[64,128]{1,0:T(8,128)}, u32[]{:S(2)}) copy-start(f32[64,128]{1,0:T(8,128)} %constant.29.clone.sin_t) | copy-start | bytes 98308
  7.5 27.8 %copy-start.5 = (f32[64,128]{1,0:T(8,128)S(1)}, f32[64,128]{1,0:T(8,128)}, u32[]{:S(2)}) copy-start(f32[64,128]{1,0:T(8,128)} %constant.28.clone.cos_t) | copy-start | bytes 98308
  7.5 27.8 %copy-start.6 = (bf16[128,64]{1,0:T(8,128)(2,1)S(1)}, bf16[128,64]{1,0:T(8,128)(2,1)}, u32[]{:S(2)}) copy-start(bf16[128,64]{1,0:T(8,128)(2,1)} %constant.21.clone.f1l) | copy-start | bytes 49156
  7.6 27.8 %copy-start.7 = (bf16[128,64]{1,0:T(8,128)(2,1)S(1)}, bf16[128,64]{1,0:T(8,128)(2,1)}, u32[]{:S(2)}) copy-start(bf16[128,64]{1,0:T(8,128)(2,1)} %constant.20.clone.f1h) | copy-start | bytes 49156
  7.6 27.8 %copy-start.8 = (bf16[64,128]{1,0:T(8,128)(2,1)S(1)}, bf16[64,128]{1,0:T(8,128)(2,1)}, u32[]{:S(2)}) copy-start(bf16[64,128]{1,0:T(8,128)(2,1)} %constant.27.clone.b1l) | copy-start | bytes 49156
  7.6 27.8 %copy-start.9 = (bf16[64,128]{1,0:T(8,128)(2,1)S(1)}, bf16[64,128]{1,0:T(8,128)(2,1)}, u32[]{:S(2)}) copy-start(bf16[64,128]{1,0:T(8,128)(2,1)} %constant.26.clone.b1h) | copy-start | bytes 49156
  7.7 27.7 %copy-start = (bf16[256,256]{1,0:T(8,128)(2,1)S(1)}, bf16[256,256]{1,0:T(8,128)(2,1)}, u32[]{:S(2)}) copy-start(bf16[256,256]{1,0:T(8,128)(2,1)} %constant.25.clone.b2l) | copy-start | bytes 393220
  7.7 27.7 %copy-start.1 = (bf16[256,256]{1,0:T(8,128)(2,1)S(1)}, bf16[256,256]{1,0:T(8,128)(2,1)}, u32[]{:S(2)}) copy-start(bf16[256,256]{1,0:T(8,128)(2,1)} %constant.24.clone.b2h) | copy-start | bytes 393220

commit v3 on v2

--- a/solution.py
+++ b/solution.py
@@ -21,7 +21,7 @@
 
 
 def trade_order(blocks):
-    first = blocks // 2 + 2 if blocks > 4 else 0
+    first = blocks * 5 // 8 + 2 if blocks > 8 else 0
     return [(first + i) % blocks for i in range(blocks)]
 
 
@@ -35,11 +35,12 @@
     cos_i, sin_i = np.cos(inner), np.sin(inner)
     outer_fwd = np.concatenate([np.cos(outer), -np.sin(outer)], axis=0)
     inner_fwd = np.block([[cos_i, -sin_i], [sin_i, cos_i]])
+    outer_back = split_table(outer_fwd.T / length)
     return (
-        *split_table(outer_fwd),
+        np.concatenate(split_table(outer_fwd), axis=0),
         *split_table(inner_fwd),
         *split_table(inner_fwd.T.copy()),
-        *split_table(outer_fwd.T / length),
+        np.block([[outer_back[0], outer_back[0]], [outer_back[1], np.zeros_like(outer_back[1])]]),
         np.cos(twist).astype(np.float32),
         np.sin(twist).astype(np.float32),
     )
@@ -53,6 +54,13 @@
 
 def dot(a, b):
     return jnp.dot(a, b, preferred_element_type=F32)
+
+
+def fine_dot(value, table_high, table_low):
+    count = value.shape[0]
+    high, low = halves(value)
+    both = dot(jnp.concatenate([high, low], axis=0), table_high)
+    return both[:count] + (both[count:] + dot(high, table_low))
 
 
 def stage_kernel(fresh, saved, top, filt, fresh_v, saved_v, top_v, filt_v, sems):
@@ -86,13 +94,12 @@
     out[...] = rows[...].astype(BF16)
 
 
-def convolve_kernel(
-    blocks, x, f1h, f1l, f2h, f2l, b2h, b2l, b1h, b1l, cos_t, sin_t, out, rows
-):
+def convolve_kernel(blocks, x, f1, f2h, f2l, b2h, b2l, b1, cos_t, sin_t, out, rows):
     rows[...] = x[...].astype(F32)
     taken = [rows[pl.ds(r, blocks, stride=8), :].astype(BF16) for r in range(8)]
     flat = jnp.concatenate(taken, axis=1)
-    first = dot(f1h[...], flat) + dot(f1l[...], flat)
+    first = dot(f1[...], flat)
+    first = first[: 2 * blocks] + first[2 * blocks :]
     width = x.shape[1]
     cosine, sine = cos_t[...], sin_t[...]
     stacked = []
@@ -102,8 +109,7 @@
         stacked.append(
             jnp.concatenate([real * cosine + imag * sine, imag * cosine - real * sine], axis=1)
         )
-    high, low = halves(jnp.concatenate(stacked, axis=0))
-    spec = dot(high, f2h[...]) + (dot(high, f2l[...]) + dot(low, f2h[...]))
+    spec = fine_dot(jnp.concatenate(stacked, axis=0), f2h[...], f2l[...])
 
     def parts_of(r):
         return (
@@ -122,8 +128,7 @@
                 (ar, ai), (br, bi) = (filt if kind == 2 else mix_b), grad
                 pair = [ar * br + ai * bi, ar * bi - ai * br]
             products.append(jnp.concatenate(pair, axis=1))
-    high, low = halves(jnp.concatenate(products, axis=0))
-    back = dot(high, b2h[...]) + (dot(high, b2l[...]) + dot(low, b2h[...]))
+    back = fine_dot(jnp.concatenate(products, axis=0), b2h[...], b2l[...])
     columns = []
     for r in range(8):
         real = back[r * blocks : (r + 1) * blocks, :width]
@@ -131,8 +136,8 @@
         columns.append(
             jnp.concatenate([real * cosine - imag * sine, imag * cosine + real * sine], axis=0)
         )
-    high, low = halves(jnp.concatenate(columns, axis=1))
-    last = dot(b1h[...], high) + (dot(b1h[...], low) + dot(b1l[...], high))
+    last = dot(b1[...], jnp.concatenate(halves(jnp.concatenate(columns, axis=1)), axis=0))
+    last = last[:blocks] + last[blocks:]
     for r in range(8):
         rows[pl.ds(r, blocks, stride=8), :] = last[:, r * width : (r + 1) * width]
     out[...] = rows[...].astype(BF16)

time: 59.4 us -> 59.1 us (level)
  no operation moved by 1% of the time
where the time goes in v3:
time: 59.1 us; the launch traced here: 58.9 us
  blocking collectives  49 us (83%)
  waiting for transfers between devices  4.11 us (7%)
  Pallas kernels  3.22 us (5%)
  starting transfers between devices  1.75 us (3%)
  between operations  0.76 us (1%)
    all_to_all x2, blocking collectives, trade(): lax.all_to_all(cut, 'seq', 0, 0, axis_index_groups=order)  49 us
    ppermute x1, waiting for transfers between devices, per_device(): returned = lax.ppermute(grad_next, 'pipe', [(b, a) for a, b in ring])  4.11 us
    ppermute x1, starting transfers between devices, per_device(): returned = lax.ppermute(grad_next, 'pipe', [(b, a) for a, b in ring])  1.73 us
    pallas_call x1, Pallas kernels, per_device(): pl.pallas_call(functools.partial(convolve_kernel, blocks), out_shape=jax....  1.4 us
  transfers between devices with their start and end apart: 2, of which 1 were waited for; matrix products, arithmetic and copies ran while one was open for 0% of the time, Pallas kernels for 2%

profile of v3, /device:TPU:6, one launch (start us, length us, event | category | flops | bytes accessed | tf_op | source)
XLA Modules:
  0.0 58.9 jit_solution(16791659394383987229)
XLA Ops:
  0.6 0.0 collective-permute-start
  0.7 1.7 %collective-permute-start.1 = (bf16[1,128,128]{2,1,0:T(8,128)(2,1)}, bf16[1,128,128]{2,1,0:T(8,128)(2,1)S(1)}, u32[]{:S(2)}, u32[]{:S(2)}) collective-permute-start(bf16[1,128,128]{2,1,0:T(8,128)(2,1)} %param.17), channel_id=1, source_target_pairs={{1,0},{2,1},{3,2},{4,3},{5,4},{6,5},{7,6},{0,7},{9,8},{10,9},{11,1... | collective-permute-start | bytes 98312 | tf_op jit(solution)/shard_map/ppermute | solution.py:179
  2.4 1.0 %stage_inputs.1 = (bf16[384,128]{1,0:T(8,128)(2,1)S(1)}, bf16[1,384,128]{2,1,0:T(8,128)(2,1)S(1)}, bf16[128,128]{1,0:T(8,128)(2,1)S(1)}, f32[1,128,128]{2,1,0:T(8,128)S(1)}) custom-call(bf16[384,128]{1,0:T(8,128)(2,1)} %fresh.1, bf16[1,384,128]{2,1,0:T(8,128)(2,1)} %saved.1, bf16[128,128]{1,0:T(8,128)(2,1)} %top.1, f32[1,128,128]{2,1,0:T(8,128)} %filt.1), custom_call_target="tpu_custom_call" | custom-call | bytes 524288 | tf_op jit(solution)/shard_map/stage_inputs/pallas_call | solution.py:184
  3.4 4.1 %collective-permute-done.1.returned = bf16[1,128,128]{2,1,0:T(8,128)(2,1)S(1)} collective-permute-done((bf16[1,128,128]{2,1,0:T(8,128)(2,1)}, bf16[1,128,128]{2,1,0:T(8,128)(2,1)S(1)}, u32[]{:S(2)}, u32[]{:S(2)}) %collective-permute-start.1) | collective-permute-done | bytes 32800 | tf_op jit(solution)/shard_map/ppermute | solution.py:179
  7.5 0.0 collective-permute-done.arrived
  7.5 0.0 copy-start.2
  7.5 0.0 copy-start.5
  7.5 0.0 copy-start.6
  7.6 0.0 copy-start.7
  7.6 0.1 gather_rows.1
  7.7 0.0 copy-start
  7.7 0.0 copy-start.1
  7.7 27.5 %all_to_all.10 = bf16[64,8,128]{2,1,0:T(8,128)(2,1)S(1)} all-to-all(bf16[64,8,128]{2,1,0:T(8,128)(2,1)S(1)} %bitcast.6), channel_id=1, replica_groups={{336,344,352,360,368,376,384,392,400,408,416,424,432,440,448,456,464,47..., dimensions={0} | all-to-all | bytes 262144 | tf_op jit(solution)/shard_map/all_to_all | solution.py:207
  35.1 0.0 copy-done.2
  35.1 0.0 copy-done.3
  35.2 0.0 copy-done.4
  35.2 0.0 copy-done.5
  35.2 0.0 copy-done.6
  35.2 0.0 copy-done.7
  35.2 0.0 copy-done
  35.2 0.0 copy-done.1
  35.2 1.4 %convolve.1 = bf16[512,128]{1,0:T(8,128)(2,1)S(1)} custom-call(bf16[512,128]{1,0:T(8,128)(2,1)S(1)} %bitcast.4, bf16[256,64]{1,0:T(8,128)(2,1)S(1)} %copy-done.5, bf16[256,256]{1,0:T(8,128)(2,1)S(1)} %copy-done.3, bf16[256,256]{1,0:T(8,128)(2,1)S(1)} %copy-done.2, bf16[256,256]{1,0:T(8,128)(2,1)S(1)} %copy-done.1, bf16[256,256]{1,0:T(8,128)(2,1)S(1)} %copy-done, ...), custom_call_target="tpu_custom_call" | custom-call | tf_op jit(solution)/shard_map/convolve/pallas_call | solution.py:210
  36.6 21.5 %all_to_all.11 = bf16[64,8,128]{2,1,0:T(8,128)(2,1)S(1)} all-to-all(bf16[64,8,128]{2,1,0:T(8,128)(2,1)S(1)} %bitcast.5), channel_id=1, replica_groups={{336,344,352,360,368,376,384,392,400,408,416,424,432,440,448,456,464,47..., dimensions={0} | all-to-all | bytes 262144 | tf_op jit(solution)/shard_map/all_to_all | solution.py:207
  58.1 0.7 %finish.1 = (bf16[1,128,128]{2,1,0:T(8,128)(2,1)}, bf16[1,384,128]{2,1,0:T(8,128)(2,1)}, f32[1,128,128]{2,1,0:T(8,128)}) custom-call(bf16[512,128]{1,0:T(8,128)(2,1)S(1)} %bitcast.7, bf16[1,384,128]{2,1,0:T(8,128)(2,1)S(1)} %collective-permute-done.arrived, bf16[384,128]{1,0:T(8,128)(2,1)S(1)} %get-tuple-element.7.fresh, ...), custom_call_target="tpu_custom_call" | custom-call | tf_op jit(solution)/shard_map/finish/pallas_call | solution.py:218
  (2 shorter events, 0.0 us)
Async XLA Ops:
  0.6 6.9 %collective-permute-start = (bf16[1,384,128]{2,1,0:T(8,128)(2,1)}, bf16[1,384,128]{2,1,0:T(8,128)(2,1)S(1)}, u32[]{:S(2)}, u32[]{:S(2)}) collective-permute-start(bf16[1,384,128]{2,1,0:T(8,128)(2,1)} %param.15), channel_id=1, source_target_pairs={{0,1},{1,2},{2,3},{3,4},{4,5},{5,6},{6,7},{7,0},{8,9},{9,10},{10,1... | collective-permute-start | bytes 294920 | tf_op jit(solution)/shard_map/ppermute | solution.py:178
  0.7 6.9 %collective-permute-start.1 = (bf16[1,128,128]{2,1,0:T(8,128)(2,1)}, bf16[1,128,128]{2,1,0:T(8,128)(2,1)S(1)}, u32[]{:S(2)}, u32[]{:S(2)}) collective-permute-start(bf16[1,128,128]{2,1,0:T(8,128)(2,1)} %param.17), channel_id=1, source_target_pairs={{1,0},{2,1},{3,2},{4,3},{5,4},{6,5},{7,6},{0,7},{9,8},{10,9},{11,1... | collective-permute-start | bytes 98312 | tf_op jit(solution)/shard_map/ppermute | solution.py:179
  7.5 27.6 %copy-start.2 = (bf16[256,256]{1,0:T(8,128)(2,1)S(1)}, bf16[256,256]{1,0:T(8,128)(2,1)}, u32[]{:S(2)}) copy-start(bf16[256,256]{1,0:T(8,128)(2,1)} %constant.18.clone.f2l) | copy-start | bytes 393220
  7.5 27.6 %copy-start.3 = (bf16[256,256]{1,0:T(8,128)(2,1)S(1)}, bf16[256,256]{1,0:T(8,128)(2,1)}, u32[]{:S(2)}) copy-start(bf16[256,256]{1,0:T(8,128)(2,1)} %constant.17.clone.f2h) | copy-start | bytes 393220
  7.5 27.6 %copy-start.4 = (bf16[128,256]{1,0:T(8,128)(2,1)S(1)}, bf16[128,256]{1,0:T(8,128)(2,1)}, u32[]{:S(2)}) copy-start(bf16[128,256]{1,0:T(8,128)(2,1)} %constant.21.clone.b1) | copy-start | bytes 196612
  7.5 27.6 %copy-start.5 = (bf16[256,64]{1,0:T(8,128)(2,1)S(1)}, bf16[256,64]{1,0:T(8,128)(2,1)}, u32[]{:S(2)}) copy-start(bf16[256,64]{1,0:T(8,128)(2,1)} %constant.16.clone.f1) | copy-start | bytes 98308
  7.5 27.6 %copy-start.6 = (f32[64,128]{1,0:T(8,128)S(1)}, f32[64,128]{1,0:T(8,128)}, u32[]{:S(2)}) copy-start(f32[64,128]{1,0:T(8,128)} %constant.23.clone.sin_t) | copy-start | bytes 98308
  7.6 27.6 %copy-start.7 = (f32[64,128]{1,0:T(8,128)S(1)}, f32[64,128]{1,0:T(8,128)}, u32[]{:S(2)}) copy-start(f32[64,128]{1,0:T(8,128)} %constant.22.clone.cos_t) | copy-start | bytes 98308
  7.7 27.5 %copy-start = (bf16[256,256]{1,0:T(8,128)(2,1)S(1)}, bf16[256,256]{1,0:T(8,128)(2,1)}, u32[]{:S(2)}) copy-start(bf16[256,256]{1,0:T(8,128)(2,1)} %constant.20.clone.b2l) | copy-start | bytes 393220
  7.7 27.5 %copy-start.1 = (bf16[256,256]{1,0:T(8,128)(2,1)S(1)}, bf16[256,256]{1,0:T(8,128)(2,1)}, u32[]{:S(2)}) copy-start(bf16[256,256]{1,0:T(8,128)(2,1)} %constant.19.clone.b2h) | copy-start | bytes 393220

commit v4 on v3

--- a/solution.py
+++ b/solution.py
@@ -21,7 +21,7 @@
 
 
 def trade_order(blocks):
-    first = blocks * 5 // 8 + 2 if blocks > 8 else 0
+    first = blocks * 11 // 16 + 2 if blocks > 8 else 0
     return [(first + i) % blocks for i in range(blocks)]
 
 
@@ -37,9 +37,9 @@
     inner_fwd = np.block([[cos_i, -sin_i], [sin_i, cos_i]])
     outer_back = split_table(outer_fwd.T / length)
     return (
-        np.concatenate(split_table(outer_fwd), axis=0),
-        *split_table(inner_fwd),
-        *split_table(inner_fwd.T.copy()),
+        np.concatenate(split_table(outer_fwd), axis=1),
+        inner_fwd.astype(ml_dtypes.bfloat16),
+        inner_fwd.T.astype(ml_dtypes.bfloat16),
         np.block([[outer_back[0], outer_back[0]], [outer_back[1], np.zeros_like(outer_back[1])]]),
         np.cos(twist).astype(np.float32),
         np.sin(twist).astype(np.float32),
@@ -56,11 +56,10 @@
     return jnp.dot(a, b, preferred_element_type=F32)
 
 
-def fine_dot(value, table_high, table_low):
+def fine_dot(value, table):
     count = value.shape[0]
-    high, low = halves(value)
-    both = dot(jnp.concatenate([high, low], axis=0), table_high)
-    return both[:count] + (both[count:] + dot(high, table_low))
+    both = dot(jnp.concatenate(halves(value), axis=0), table)
+    return both[:count] + both[count:]
 
 
 def stage_kernel(fresh, saved, top, filt, fresh_v, saved_v, top_v, filt_v, sems):
@@ -94,12 +93,11 @@
     out[...] = rows[...].astype(BF16)
 
 
-def convolve_kernel(blocks, x, f1, f2h, f2l, b2h, b2l, b1, cos_t, sin_t, out, rows):
+def convolve_kernel(blocks, x, f1, f2, b2, b1, cos_t, sin_t, out, rows):
     rows[...] = x[...].astype(F32)
     taken = [rows[pl.ds(r, blocks, stride=8), :].astype(BF16) for r in range(8)]
     flat = jnp.concatenate(taken, axis=1)
-    first = dot(f1[...], flat)
-    first = first[: 2 * blocks] + first[2 * blocks :]
+    first = dot(f1[...], jnp.concatenate([flat, flat], axis=0))
     width = x.shape[1]
     cosine, sine = cos_t[...], sin_t[...]
     stacked = []
@@ -109,7 +107,7 @@
         stacked.append(
             jnp.concatenate([real * cosine + imag * sine, imag * cosine - real * sine], axis=1)
         )
-    spec = fine_dot(jnp.concatenate(stacked, axis=0), f2h[...], f2l[...])
+    spec = fine_dot(jnp.concatenate(stacked, axis=0), f2[...])
 
     def parts_of(r):
         return (
@@ -128,7 +126,7 @@
                 (ar, ai), (br, bi) = (filt if kind == 2 else mix_b), grad
                 pair = [ar * br + ai * bi, ar * bi - ai * br]
             products.append(jnp.concatenate(pair, axis=1))
-    back = fine_dot(jnp.concatenate(products, axis=0), b2h[...], b2l[...])
+    back = fine_dot(jnp.concatenate(products, axis=0), b2[...])
     columns = []
     for r in range(8):
         real = back[r * blocks : (r + 1) * blocks, :width]

time: 59.1 us -> 58.4 us (0.988)
  no operation moved by 1% of the time
where the time goes in v4:
time: 58.4 us; the launch traced here: 58.2 us
  blocking collectives  48.7 us (83%)
  waiting for transfers between devices  4.11 us (7%)
  Pallas kernels  2.94 us (5%)
  starting transfers between devices  1.75 us (3%)
  between operations  0.72 us (1%)
    all_to_all x2, blocking collectives, trade(): lax.all_to_all(cut, 'seq', 0, 0, axis_index_groups=order)  48.7 us
    ppermute x1, waiting for transfers between devices, per_device(): returned = lax.ppermute(grad_next, 'pipe', [(b, a) for a, b in ring])  4.11 us
    ppermute x1, starting transfers between devices, per_device(): returned = lax.ppermute(grad_next, 'pipe', [(b, a) for a, b in ring])  1.73 us
  transfers between devices with their start and end apart: 2, of which 1 were waited for; matrix products, arithmetic and copies ran while one was open for 0% of the time, Pallas kernels for 2%

profile of v4, /device:TPU:6, one launch (start us, length us, event | category | flops | bytes accessed | tf_op | source)
XLA Modules:
  0.0 58.2 jit_solution(7207044975802536057)
XLA Ops:
  0.6 0.0 collective-permute-start
  0.7 1.7 %collective-permute-start.1 = (bf16[1,128,128]{2,1,0:T(8,128)(2,1)}, bf16[1,128,128]{2,1,0:T(8,128)(2,1)S(1)}, u32[]{:S(2)}, u32[]{:S(2)}) collective-permute-start(bf16[1,128,128]{2,1,0:T(8,128)(2,1)} %param.15), channel_id=1, source_target_pairs={{1,0},{2,1},{3,2},{4,3},{5,4},{6,5},{7,6},{0,7},{9,8},{10,9},{11,1... | collective-permute-start | bytes 98312 | tf_op jit(solution)/shard_map/ppermute | solution.py:177
  2.4 1.0 %stage_inputs.1 = (bf16[384,128]{1,0:T(8,128)(2,1)S(1)}, bf16[1,384,128]{2,1,0:T(8,128)(2,1)S(1)}, bf16[128,128]{1,0:T(8,128)(2,1)S(1)}, f32[1,128,128]{2,1,0:T(8,128)S(1)}) custom-call(bf16[384,128]{1,0:T(8,128)(2,1)} %fresh.1, bf16[1,384,128]{2,1,0:T(8,128)(2,1)} %saved.1, bf16[128,128]{1,0:T(8,128)(2,1)} %top.1, f32[1,128,128]{2,1,0:T(8,128)} %filt.1), custom_call_target="tpu_custom_call" | custom-call | bytes 524288 | tf_op jit(solution)/shard_map/stage_inputs/pallas_call | solution.py:182
  3.4 4.1 %collective-permute-done.1.returned = bf16[1,128,128]{2,1,0:T(8,128)(2,1)S(1)} collective-permute-done((bf16[1,128,128]{2,1,0:T(8,128)(2,1)}, bf16[1,128,128]{2,1,0:T(8,128)(2,1)S(1)}, u32[]{:S(2)}, u32[]{:S(2)}) %collective-permute-start.1) | collective-permute-done | bytes 32800 | tf_op jit(solution)/shard_map/ppermute | solution.py:177
  7.5 0.0 collective-permute-done.arrived
  7.5 0.0 copy-start.2
  7.5 0.0 copy-start.3
  7.5 0.0 copy-start.4
  7.5 0.0 copy-start.5
  7.5 0.1 gather_rows.1
  7.6 0.0 copy-start
  7.7 0.0 copy-start.1
  7.7 27.5 %all_to_all.10 = bf16[64,8,128]{2,1,0:T(8,128)(2,1)S(1)} all-to-all(bf16[64,8,128]{2,1,0:T(8,128)(2,1)S(1)} %bitcast.4), channel_id=1, replica_groups={{368,376,384,392,400,408,416,424,432,440,448,456,464,472,480,488,496,50..., dimensions={0} | all-to-all | bytes 262144 | tf_op jit(solution)/shard_map/all_to_all | solution.py:205
  35.1 0.0 copy-done.2
  35.1 0.0 copy-done.3
  35.1 0.0 copy-done.4
  35.1 0.0 copy-done.5
  35.1 0.0 copy-done
  35.2 0.0 copy-done.1
  35.2 1.1 %convolve.1 = bf16[512,128]{1,0:T(8,128)(2,1)S(1)} custom-call(bf16[512,128]{1,0:T(8,128)(2,1)S(1)} %bitcast.6, bf16[128,128]{1,0:T(8,128)(2,1)S(1)} %copy-done.5, bf16[256,256]{1,0:T(8,128)(2,1)S(1)} %copy-done.1, bf16[256,256]{1,0:T(8,128)(2,1)S(1)} %copy-done, bf16[128,256]{1,0:T(8,128)(2,1)S(1)} %copy-done.2, f32[64,128]{1,0:T(8,128)S(1)} %copy-done.4, ...), custom_call_target="tpu_custom_call" | custom-call | tf_op jit(solution)/shard_map/convolve/pallas_call | solution.py:208
  36.3 21.2 %all_to_all.11 = bf16[64,8,128]{2,1,0:T(8,128)(2,1)S(1)} all-to-all(bf16[64,8,128]{2,1,0:T(8,128)(2,1)S(1)} %bitcast.7), channel_id=1, replica_groups={{368,376,384,392,400,408,416,424,432,440,448,456,464,472,480,488,496,50..., dimensions={0} | all-to-all | bytes 262144 | tf_op jit(solution)/shard_map/all_to_all | solution.py:205
  57.5 0.7 %finish.1 = (bf16[1,128,128]{2,1,0:T(8,128)(2,1)}, bf16[1,384,128]{2,1,0:T(8,128)(2,1)}, f32[1,128,128]{2,1,0:T(8,128)}) custom-call(bf16[512,128]{1,0:T(8,128)(2,1)S(1)} %bitcast.5, bf16[1,384,128]{2,1,0:T(8,128)(2,1)S(1)} %collective-permute-done.arrived, bf16[384,128]{1,0:T(8,128)(2,1)S(1)} %get-tuple-element.7.fresh, ...), custom_call_target="tpu_custom_call" | custom-call | tf_op jit(solution)/shard_map/finish/pallas_call | solution.py:216
Async XLA Ops:
  0.6 6.9 %collective-permute-start = (bf16[1,384,128]{2,1,0:T(8,128)(2,1)}, bf16[1,384,128]{2,1,0:T(8,128)(2,1)S(1)}, u32[]{:S(2)}, u32[]{:S(2)}) collective-permute-start(bf16[1,384,128]{2,1,0:T(8,128)(2,1)} %param.13), channel_id=1, source_target_pairs={{0,1},{1,2},{2,3},{3,4},{4,5},{5,6},{6,7},{7,0},{8,9},{9,10},{10,1... | collective-permute-start | bytes 294920 | tf_op jit(solution)/shard_map/ppermute | solution.py:176
  0.7 6.9 %collective-permute-start.1 = (bf16[1,128,128]{2,1,0:T(8,128)(2,1)}, bf16[1,128,128]{2,1,0:T(8,128)(2,1)S(1)}, u32[]{:S(2)}, u32[]{:S(2)}) collective-permute-start(bf16[1,128,128]{2,1,0:T(8,128)(2,1)} %param.15), channel_id=1, source_target_pairs={{1,0},{2,1},{3,2},{4,3},{5,4},{6,5},{7,6},{0,7},{9,8},{10,9},{11,1... | collective-permute-start | bytes 98312 | tf_op jit(solution)/shard_map/ppermute | solution.py:177
  7.5 27.6 %copy-start.2 = (bf16[128,256]{1,0:T(8,128)(2,1)S(1)}, bf16[128,256]{1,0:T(8,128)(2,1)}, u32[]{:S(2)}) copy-start(bf16[128,256]{1,0:T(8,128)(2,1)} %constant.15.clone.b1) | copy-start | bytes 196612
  7.5 27.6 %copy-start.3 = (f32[64,128]{1,0:T(8,128)S(1)}, f32[64,128]{1,0:T(8,128)}, u32[]{:S(2)}) copy-start(f32[64,128]{1,0:T(8,128)} %constant.17.clone.sin_t) | copy-start | bytes 98308
  7.5 27.6 %copy-start.4 = (f32[64,128]{1,0:T(8,128)S(1)}, f32[64,128]{1,0:T(8,128)}, u32[]{:S(2)}) copy-start(f32[64,128]{1,0:T(8,128)} %constant.16.clone.cos_t) | copy-start | bytes 98308
  7.5 27.6 %copy-start.5 = (bf16[128,128]{1,0:T(8,128)(2,1)S(1)}, bf16[128,128]{1,0:T(8,128)(2,1)}, u32[]{:S(2)}) copy-start(bf16[128,128]{1,0:T(8,128)(2,1)} %constant.12.clone.f1) | copy-start | bytes 98308
  7.6 27.5 %copy-start = (bf16[256,256]{1,0:T(8,128)(2,1)S(1)}, bf16[256,256]{1,0:T(8,128)(2,1)}, u32[]{:S(2)}) copy-start(bf16[256,256]{1,0:T(8,128)(2,1)} %constant.14.clone.b2) | copy-start | bytes 393220
  7.7 27.5 %copy-start.1 = (bf16[256,256]{1,0:T(8,128)(2,1)S(1)}, bf16[256,256]{1,0:T(8,128)(2,1)}, u32[]{:S(2)}) copy-start(bf16[256,256]{1,0:T(8,128)(2,1)} %constant.13.clone.f2) | copy-start | bytes 393220

commit v5 on v4

--- a/solution.py
+++ b/solution.py
@@ -22,7 +22,8 @@
 
 def trade_order(blocks):
     first = blocks * 11 // 16 + 2 if blocks > 8 else 0
-    return [(first + i) % blocks for i in range(blocks)]
+    away = [min((i - first) % blocks, (first - i) % blocks) for i in range(blocks)]
+    return sorted(range(blocks), key=lambda i: (i != first, -away[i], i))
 
 
 @functools.lru_cache(maxsize=None)

time: 58.4 us -> 58.3 us (level)
  no operation moved by 1% of the time
where the time goes in v5:
time: 58.3 us; the launch traced here: 58.1 us
  blocking collectives  48.6 us (83%)
  waiting for transfers between devices  4.11 us (7%)
  Pallas kernels  2.94 us (5%)
  starting transfers between devices  1.75 us (3%)
  between operations  0.72 us (1%)
    all_to_all x2, blocking collectives, trade(): lax.all_to_all(cut, 'seq', 0, 0, axis_index_groups=order)  48.6 us
    ppermute x1, waiting for transfers between devices, per_device(): returned = lax.ppermute(grad_next, 'pipe', [(b, a) for a, b in ring])  4.11 us
    ppermute x1, starting transfers between devices, per_device(): returned = lax.ppermute(grad_next, 'pipe', [(b, a) for a, b in ring])  1.73 us
  transfers between devices with their start and end apart: 2, of which 1 were waited for; matrix products, arithmetic and copies ran while one was open for 0% of the time, Pallas kernels for 2%

profile of v5, /device:TPU:6, one launch (start us, length us, event | category | flops | bytes accessed | tf_op | source)
XLA Modules:
  0.0 58.1 jit_solution(4880241522330833156)
XLA Ops:
  0.6 0.0 collective-permute-start
  0.7 1.7 %collective-permute-start.1 = (bf16[1,128,128]{2,1,0:T(8,128)(2,1)}, bf16[1,128,128]{2,1,0:T(8,128)(2,1)S(1)}, u32[]{:S(2)}, u32[]{:S(2)}) collective-permute-start(bf16[1,128,128]{2,1,0:T(8,128)(2,1)} %param.15), channel_id=1, source_target_pairs={{1,0},{2,1},{3,2},{4,3},{5,4},{6,5},{7,6},{0,7},{9,8},{10,9},{11,1... | collective-permute-start | bytes 98312 | tf_op jit(solution)/shard_map/ppermute | solution.py:178
  2.4 1.0 %stage_inputs.1 = (bf16[384,128]{1,0:T(8,128)(2,1)S(1)}, bf16[1,384,128]{2,1,0:T(8,128)(2,1)S(1)}, bf16[128,128]{1,0:T(8,128)(2,1)S(1)}, f32[1,128,128]{2,1,0:T(8,128)S(1)}) custom-call(bf16[384,128]{1,0:T(8,128)(2,1)} %fresh.1, bf16[1,384,128]{2,1,0:T(8,128)(2,1)} %saved.1, bf16[128,128]{1,0:T(8,128)(2,1)} %top.1, f32[1,128,128]{2,1,0:T(8,128)} %filt.1), custom_call_target="tpu_custom_call" | custom-call | bytes 524288 | tf_op jit(solution)/shard_map/stage_inputs/pallas_call | solution.py:183
  3.4 4.1 %collective-permute-done.1.returned = bf16[1,128,128]{2,1,0:T(8,128)(2,1)S(1)} collective-permute-done((bf16[1,128,128]{2,1,0:T(8,128)(2,1)}, bf16[1,128,128]{2,1,0:T(8,128)(2,1)S(1)}, u32[]{:S(2)}, u32[]{:S(2)}) %collective-permute-start.1) | collective-permute-done | bytes 32800 | tf_op jit(solution)/shard_map/ppermute | solution.py:178
  7.5 0.0 collective-permute-done.arrived
  7.5 0.0 copy-start.2
  7.5 0.0 copy-start.3
  7.5 0.0 copy-start.4
  7.5 0.0 copy-start.5
  7.5 0.1 gather_rows.1
  7.6 0.0 copy-start
  7.7 0.0 copy-start.1
  7.7 27.3 %all_to_all.10 = bf16[64,8,128]{2,1,0:T(8,128)(2,1)S(1)} all-to-all(bf16[64,8,128]{2,1,0:T(8,128)(2,1)S(1)} %bitcast.4), channel_id=1, replica_groups={{368,112,104,120,96,128,88,136,80,144,72,152,64,160,56,168,48,176,40,18..., dimensions={0} | all-to-all | bytes 262144 | tf_op jit(solution)/shard_map/all_to_all | solution.py:206
  35.0 0.0 copy-done.2
  35.0 0.0 copy-done.3
  35.0 0.0 copy-done.4
  35.0 0.0 copy-done.5
  35.0 0.0 copy-done
  35.0 0.0 copy-done.1
  35.0 1.1 %convolve.1 = bf16[512,128]{1,0:T(8,128)(2,1)S(1)} custom-call(bf16[512,128]{1,0:T(8,128)(2,1)S(1)} %bitcast.6, bf16[128,128]{1,0:T(8,128)(2,1)S(1)} %copy-done.5, bf16[256,256]{1,0:T(8,128)(2,1)S(1)} %copy-done.1, bf16[256,256]{1,0:T(8,128)(2,1)S(1)} %copy-done, bf16[128,256]{1,0:T(8,128)(2,1)S(1)} %copy-done.2, f32[64,128]{1,0:T(8,128)S(1)} %copy-done.4, ...), custom_call_target="tpu_custom_call" | custom-call | tf_op jit(solution)/shard_map/convolve/pallas_call | solution.py:209
  36.2 21.2 %all_to_all.11 = bf16[64,8,128]{2,1,0:T(8,128)(2,1)S(1)} all-to-all(bf16[64,8,128]{2,1,0:T(8,128)(2,1)S(1)} %bitcast.7), channel_id=1, replica_groups={{368,112,104,120,96,128,88,136,80,144,72,152,64,160,56,168,48,176,40,18..., dimensions={0} | all-to-all | bytes 262144 | tf_op jit(solution)/shard_map/all_to_all | solution.py:206
  57.4 0.7 %finish.1 = (bf16[1,128,128]{2,1,0:T(8,128)(2,1)}, bf16[1,384,128]{2,1,0:T(8,128)(2,1)}, f32[1,128,128]{2,1,0:T(8,128)}) custom-call(bf16[512,128]{1,0:T(8,128)(2,1)S(1)} %bitcast.5, bf16[1,384,128]{2,1,0:T(8,128)(2,1)S(1)} %collective-permute-done.arrived, bf16[384,128]{1,0:T(8,128)(2,1)S(1)} %get-tuple-element.7.fresh, ...), custom_call_target="tpu_custom_call" | custom-call | tf_op jit(solution)/shard_map/finish/pallas_call | solution.py:217
Async XLA Ops:
  0.6 6.9 %collective-permute-start = (bf16[1,384,128]{2,1,0:T(8,128)(2,1)}, bf16[1,384,128]{2,1,0:T(8,128)(2,1)S(1)}, u32[]{:S(2)}, u32[]{:S(2)}) collective-permute-start(bf16[1,384,128]{2,1,0:T(8,128)(2,1)} %param.13), channel_id=1, source_target_pairs={{0,1},{1,2},{2,3},{3,4},{4,5},{5,6},{6,7},{7,0},{8,9},{9,10},{10,1... | collective-permute-start | bytes 294920 | tf_op jit(solution)/shard_map/ppermute | solution.py:177
  0.7 6.9 %collective-permute-start.1 = (bf16[1,128,128]{2,1,0:T(8,128)(2,1)}, bf16[1,128,128]{2,1,0:T(8,128)(2,1)S(1)}, u32[]{:S(2)}, u32[]{:S(2)}) collective-permute-start(bf16[1,128,128]{2,1,0:T(8,128)(2,1)} %param.15), channel_id=1, source_target_pairs={{1,0},{2,1},{3,2},{4,3},{5,4},{6,5},{7,6},{0,7},{9,8},{10,9},{11,1... | collective-permute-start | bytes 98312 | tf_op jit(solution)/shard_map/ppermute | solution.py:178
  7.5 27.5 %copy-start.2 = (bf16[128,256]{1,0:T(8,128)(2,1)S(1)}, bf16[128,256]{1,0:T(8,128)(2,1)}, u32[]{:S(2)}) copy-start(bf16[128,256]{1,0:T(8,128)(2,1)} %constant.15.clone.b1) | copy-start | bytes 196612
  7.5 27.5 %copy-start.3 = (f32[64,128]{1,0:T(8,128)S(1)}, f32[64,128]{1,0:T(8,128)}, u32[]{:S(2)}) copy-start(f32[64,128]{1,0:T(8,128)} %constant.17.clone.sin_t) | copy-start | bytes 98308
  7.5 27.5 %copy-start.4 = (f32[64,128]{1,0:T(8,128)S(1)}, f32[64,128]{1,0:T(8,128)}, u32[]{:S(2)}) copy-start(f32[64,128]{1,0:T(8,128)} %constant.16.clone.cos_t) | copy-start | bytes 98308
  7.5 27.5 %copy-start.5 = (bf16[128,128]{1,0:T(8,128)(2,1)S(1)}, bf16[128,128]{1,0:T(8,128)(2,1)}, u32[]{:S(2)}) copy-start(bf16[128,128]{1,0:T(8,128)(2,1)} %constant.12.clone.f1) | copy-start | bytes 98308
  7.6 27.4 %copy-start = (bf16[256,256]{1,0:T(8,128)(2,1)S(1)}, bf16[256,256]{1,0:T(8,128)(2,1)}, u32[]{:S(2)}) copy-start(bf16[256,256]{1,0:T(8,128)(2,1)} %constant.14.clone.b2) | copy-start | bytes 393220
  7.7 27.4 %copy-start.1 = (bf16[256,256]{1,0:T(8,128)(2,1)S(1)}, bf16[256,256]{1,0:T(8,128)(2,1)}, u32[]{:S(2)}) copy-start(bf16[256,256]{1,0:T(8,128)(2,1)} %constant.13.clone.f2) | copy-start | bytes 393220

commit v6 on v5

--- a/solution.py
+++ b/solution.py
@@ -21,7 +21,7 @@
 
 
 def trade_order(blocks):
-    first = blocks * 11 // 16 + 2 if blocks > 8 else 0
+    first = blocks * 11 // 16 + 3 if blocks > 8 else 0
     away = [min((i - first) % blocks, (first - i) % blocks) for i in range(blocks)]
     return sorted(range(blocks), key=lambda i: (i != first, -away[i], i))
 

time: 58.3 us -> 58.7 us (level)
  no operation moved by 1% of the time
where the time goes in v6:
time: 58.7 us; the launch traced here: 58.4 us
  blocking collectives  48.9 us (83%)
  waiting for transfers between devices  4.11 us (7%)
  Pallas kernels  2.94 us (5%)
  starting transfers between devices  1.75 us (3%)
  between operations  0.72 us (1%)
    all_to_all x2, blocking collectives, trade(): lax.all_to_all(cut, 'seq', 0, 0, axis_index_groups=order)  48.9 us
    ppermute x1, waiting for transfers between devices, per_device(): returned = lax.ppermute(grad_next, 'pipe', [(b, a) for a, b in ring])  4.11 us
    ppermute x1, starting transfers between devices, per_device(): returned = lax.ppermute(grad_next, 'pipe', [(b, a) for a, b in ring])  1.73 us
  transfers between devices with their start and end apart: 2, of which 1 were waited for; matrix products, arithmetic and copies ran while one was open for 0% of the time, Pallas kernels for 2%

profile of v6, /device:TPU:6, one launch (start us, length us, event | category | flops | bytes accessed | tf_op | source)
XLA Modules:
  0.0 58.4 jit_solution(18185187057274870636)
XLA Ops:
  0.6 0.0 collective-permute-start
  0.7 1.7 %collective-permute-start.1 = (bf16[1,128,128]{2,1,0:T(8,128)(2,1)}, bf16[1,128,128]{2,1,0:T(8,128)(2,1)S(1)}, u32[]{:S(2)}, u32[]{:S(2)}) collective-permute-start(bf16[1,128,128]{2,1,0:T(8,128)(2,1)} %param.15), channel_id=1, source_target_pairs={{1,0},{2,1},{3,2},{4,3},{5,4},{6,5},{7,6},{0,7},{9,8},{10,9},{11,1... | collective-permute-start | bytes 98312 | tf_op jit(solution)/shard_map/ppermute | solution.py:178
  2.4 1.0 %stage_inputs.1 = (bf16[384,128]{1,0:T(8,128)(2,1)S(1)}, bf16[1,384,128]{2,1,0:T(8,128)(2,1)S(1)}, bf16[128,128]{1,0:T(8,128)(2,1)S(1)}, f32[1,128,128]{2,1,0:T(8,128)S(1)}) custom-call(bf16[384,128]{1,0:T(8,128)(2,1)} %fresh.1, bf16[1,384,128]{2,1,0:T(8,128)(2,1)} %saved.1, bf16[128,128]{1,0:T(8,128)(2,1)} %top.1, f32[1,128,128]{2,1,0:T(8,128)} %filt.1), custom_call_target="tpu_custom_call" | custom-call | bytes 524288 | tf_op jit(solution)/shard_map/stage_inputs/pallas_call | solution.py:183
  3.4 4.1 %collective-permute-done.1.returned = bf16[1,128,128]{2,1,0:T(8,128)(2,1)S(1)} collective-permute-done((bf16[1,128,128]{2,1,0:T(8,128)(2,1)}, bf16[1,128,128]{2,1,0:T(8,128)(2,1)S(1)}, u32[]{:S(2)}, u32[]{:S(2)}) %collective-permute-start.1) | collective-permute-done | bytes 32800 | tf_op jit(solution)/shard_map/ppermute | solution.py:178
  7.5 0.0 collective-permute-done.arrived
  7.5 0.0 copy-start.2
  7.5 0.0 copy-start.3
  7.5 0.0 copy-start.4
  7.5 0.0 copy-start.5
  7.5 0.1 gather_rows.1
  7.6 0.0 copy-start
  7.7 0.0 copy-start.1
  7.7 26.9 %all_to_all.10 = bf16[64,8,128]{2,1,0:T(8,128)(2,1)S(1)} all-to-all(bf16[64,8,128]{2,1,0:T(8,128)(2,1)S(1)} %bitcast.4), channel_id=1, replica_groups={{376,120,112,128,104,136,96,144,88,152,80,160,72,168,64,176,56,184,48,1..., dimensions={0} | all-to-all | bytes 262144 | tf_op jit(solution)/shard_map/all_to_all | solution.py:206
  34.5 0.0 copy-done.2
  34.5 0.0 copy-done.3
  34.6 0.0 copy-done.4
  34.6 0.0 copy-done.5
  34.6 0.0 copy-done
  34.6 0.0 copy-done.1
  34.6 1.1 %convolve.1 = bf16[512,128]{1,0:T(8,128)(2,1)S(1)} custom-call(bf16[512,128]{1,0:T(8,128)(2,1)S(1)} %bitcast.6, bf16[128,128]{1,0:T(8,128)(2,1)S(1)} %copy-done.5, bf16[256,256]{1,0:T(8,128)(2,1)S(1)} %copy-done.1, bf16[256,256]{1,0:T(8,128)(2,1)S(1)} %copy-done, bf16[128,256]{1,0:T(8,128)(2,1)S(1)} %copy-done.2, f32[64,128]{1,0:T(8,128)S(1)} %copy-done.4, ...), custom_call_target="tpu_custom_call" | custom-call | tf_op jit(solution)/shard_map/convolve/pallas_call | solution.py:209
  35.7 22.0 %all_to_all.11 = bf16[64,8,128]{2,1,0:T(8,128)(2,1)S(1)} all-to-all(bf16[64,8,128]{2,1,0:T(8,128)(2,1)S(1)} %bitcast.7), channel_id=1, replica_groups={{376,120,112,128,104,136,96,144,88,152,80,160,72,168,64,176,56,184,48,1..., dimensions={0} | all-to-all | bytes 262144 | tf_op jit(solution)/shard_map/all_to_all | solution.py:206
  57.7 0.7 %finish.1 = (bf16[1,128,128]{2,1,0:T(8,128)(2,1)}, bf16[1,384,128]{2,1,0:T(8,128)(2,1)}, f32[1,128,128]{2,1,0:T(8,128)}) custom-call(bf16[512,128]{1,0:T(8,128)(2,1)S(1)} %bitcast.5, bf16[1,384,128]{2,1,0:T(8,128)(2,1)S(1)} %collective-permute-done.arrived, bf16[384,128]{1,0:T(8,128)(2,1)S(1)} %get-tuple-element.7.fresh, ...), custom_call_target="tpu_custom_call" | custom-call | tf_op jit(solution)/shard_map/finish/pallas_call | solution.py:217
Async XLA Ops:
  0.6 6.9 %collective-permute-start = (bf16[1,384,128]{2,1,0:T(8,128)(2,1)}, bf16[1,384,128]{2,1,0:T(8,128)(2,1)S(1)}, u32[]{:S(2)}, u32[]{:S(2)}) collective-permute-start(bf16[1,384,128]{2,1,0:T(8,128)(2,1)} %param.13), channel_id=1, source_target_pairs={{0,1},{1,2},{2,3},{3,4},{4,5},{5,6},{6,7},{7,0},{8,9},{9,10},{10,1... | collective-permute-start | bytes 294920 | tf_op jit(solution)/shard_map/ppermute | solution.py:177
  0.7 6.9 %collective-permute-start.1 = (bf16[1,128,128]{2,1,0:T(8,128)(2,1)}, bf16[1,128,128]{2,1,0:T(8,128)(2,1)S(1)}, u32[]{:S(2)}, u32[]{:S(2)}) collective-permute-start(bf16[1,128,128]{2,1,0:T(8,128)(2,1)} %param.15), channel_id=1, source_target_pairs={{1,0},{2,1},{3,2},{4,3},{5,4},{6,5},{7,6},{0,7},{9,8},{10,9},{11,1... | collective-permute-start | bytes 98312 | tf_op jit(solution)/shard_map/ppermute | solution.py:178
  7.5 27.0 %copy-start.2 = (bf16[128,256]{1,0:T(8,128)(2,1)S(1)}, bf16[128,256]{1,0:T(8,128)(2,1)}, u32[]{:S(2)}) copy-start(bf16[128,256]{1,0:T(8,128)(2,1)} %constant.15.clone.b1) | copy-start | bytes 196612
  7.5 27.0 %copy-start.3 = (f32[64,128]{1,0:T(8,128)S(1)}, f32[64,128]{1,0:T(8,128)}, u32[]{:S(2)}) copy-start(f32[64,128]{1,0:T(8,128)} %constant.17.clone.sin_t) | copy-start | bytes 98308
  7.5 27.0 %copy-start.4 = (f32[64,128]{1,0:T(8,128)S(1)}, f32[64,128]{1,0:T(8,128)}, u32[]{:S(2)}) copy-start(f32[64,128]{1,0:T(8,128)} %constant.16.clone.cos_t) | copy-start | bytes 98308
  7.5 27.0 %copy-start.5 = (bf16[128,128]{1,0:T(8,128)(2,1)S(1)}, bf16[128,128]{1,0:T(8,128)(2,1)}, u32[]{:S(2)}) copy-start(bf16[128,128]{1,0:T(8,128)(2,1)} %constant.12.clone.f1) | copy-start | bytes 98308
  7.6 26.9 %copy-start = (bf16[256,256]{1,0:T(8,128)(2,1)S(1)}, bf16[256,256]{1,0:T(8,128)(2,1)}, u32[]{:S(2)}) copy-start(bf16[256,256]{1,0:T(8,128)(2,1)} %constant.14.clone.b2) | copy-start | bytes 393220
  7.7 26.9 %copy-start.1 = (bf16[256,256]{1,0:T(8,128)(2,1)S(1)}, bf16[256,256]{1,0:T(8,128)(2,1)}, u32[]{:S(2)}) copy-start(bf16[256,256]{1,0:T(8,128)(2,1)} %constant.13.clone.f2) | copy-start | bytes 393220
